TPU v7x, 512 devices: a whole 4x4x16 slice. The times are simulated.
512 devices in a mesh: fsdp: 64 (over z, x_hi, core), tp: 8 (over y, x_lo).
Axes of the slice: x: 4 (x_hi: 2, x_lo: 2; x = x_hi * 2 + x_lo), y: 4, z: 16, core: 2. Of those that a mesh axis runs over, the one named last changes fastest.
Arguments:
- token_ids: int32 [256, 2], P('fsdp'), may hold values from 0 to 81919
- cache_lengths: int32 [256], P('fsdp'), may hold values from 256 to 1022, as said below
- embedding: bfloat16 [81920, 5120], P('fsdp', 'tp'), may hold values from -6 to 6
- norm_gain: bfloat16 [5120], replicated, may hold values from 0.099609375 to 1.8984375
- key_norm_gain: bfloat16 [128], replicated, may hold values from 0.099609375 to 1.8984375
- key_weight: float32 [5120, 1024], P(('fsdp', 'tp')), may hold values from -0.078125 to 0.078125
- key_grad: float32 [5120, 1024], P(('fsdp', 'tp')), may hold values from -12 to 12
- key_first: float32 [5120, 1024], P(('fsdp', 'tp')), may hold values from -1.2 to 1.2
- key_second: float32 [5120, 1024], P(('fsdp', 'tp')), may hold values from 0.5 to 8
- value_weight: float32 [5120, 1024], P(('fsdp', 'tp')), may hold values from -0.078125 to 0.078125
- value_grad: float32 [5120, 1024], P(('fsdp', 'tp')), may hold values from -12 to 12
- value_first: float32 [5120, 1024], P(('fsdp', 'tp')), may hold values from -1.2 to 1.2
- value_second: float32 [5120, 1024], P(('fsdp', 'tp')), may hold values from 0.5 to 8
- queries: bfloat16 [256, 2, 8192], P('fsdp', None, 'tp'), may hold values from -7 to 7
- key_cache: bfloat16 [256, 8, 1024, 128], P('fsdp', 'tp'), may hold values from -7 to 7
- cached_value_rows: bfloat16 [256, 8, 1024, 128], P('fsdp', 'tp'), may hold values from -6 to 6
Outputs:
- attention: bfloat16 [256, 2, 8192], P('fsdp', None, 'tp')
- new_key_weight: float32 [5120, 1024], P(('fsdp', 'tp'))
- new_key_first: float32 [5120, 1024], P(('fsdp', 'tp'))
- new_key_second: float32 [5120, 1024], P(('fsdp', 'tp'))
- new_value_weight: float32 [5120, 1024], P(('fsdp', 'tp'))
- new_value_first: float32 [5120, 1024], P(('fsdp', 'tp'))
- new_value_second: float32 [5120, 1024], P(('fsdp', 'tp'))
Inputs may be any that keep to these rules, and one draw needn't show every extreme that they name: `cache_lengths`: cache entries at and above a rollout's length are unused; some rollout reaches the largest length.
All inputs are finite; a program needn't handle non-finite values.
Results may differ from a plain program's by a relative error of at most 0.0049.
Values may be sent and summed in bfloat16 or wider, within the bound.
No kernel may reach another device: no remote copies, remote signals or barrier semaphores. Data moves between devices by JAX's collectives and lax.ppermute only.
A program may use at most 64 MiB of HBM per device.

v0:
```python
import jax
import jax.numpy as jnp
from jax import lax
from jax.sharding import PartitionSpec as P

HEAD_SIZE = 128


beta_one = 0.9
beta_two = 0.95
learn_rate = 0.001
weight_decay = 0.1
adam_eps = 1e-08
norm_eps = 1e-06
rope_base = 1000000.0


def adamw(weight, gradient, moment_one, moment_two):
    first_new = beta_one * moment_one + (1.0 - beta_one) * gradient
    second_new = beta_two * moment_two + (1.0 - beta_two) * gradient * gradient
    correct_one = 1.0 - beta_one**50
    correct_two = 1.0 - beta_two**50
    update = (
        first_new / correct_one / (jnp.sqrt(second_new / correct_two) + adam_eps)
        + weight_decay * weight
    )
    return (weight - learn_rate * update, first_new, second_new)


def rotate(vectors, positions):
    half_width = vectors.shape[-1] // 2
    frequency = rope_base ** (-jnp.arange(half_width, dtype=jnp.float32) * 2.0 / vectors.shape[-1])
    angles = positions[..., None] * frequency
    cosine = jnp.cos(angles)
    sine = jnp.sin(angles)
    upper_half = vectors[..., :half_width]
    lower_half = vectors[..., half_width:]
    return jnp.concatenate(
        [upper_half * cosine - lower_half * sine, lower_half * cosine + upper_half * sine], axis=-1
    )


def body(
    token_ids,
    cache_lengths,
    embedding,
    norm_gain,
    key_norm_gain,
    key_weight,
    key_grad,
    key_first,
    key_second,
    value_weight,
    value_grad,
    value_first,
    value_second,
    queries,
    key_cache,
    cached_value_rows,
):
    new_key_weight, new_key_first, new_key_second = adamw(
        key_weight, key_grad, key_first, key_second
    )
    new_value_weight, new_value_first, new_value_second = adamw(
        value_weight, value_grad, value_first, value_second
    )
    head_key, head_value = (
        lax.all_to_all(
            new_key_weight.astype(jnp.bfloat16), "tp", split_axis=1, concat_axis=0, tiled=True
        ),
        lax.all_to_all(
            new_value_weight.astype(jnp.bfloat16), "tp", split_axis=1, concat_axis=0, tiled=True
        ),
    )
    vocab_rows = embedding.shape[0]
    all_ids = lax.all_gather(token_ids, "fsdp", axis=0, tiled=True).reshape(-1)
    local_ids = all_ids - lax.axis_index("fsdp") * vocab_rows
    vocab_index = jnp.arange(vocab_rows, dtype=jnp.int32)
    onehot = (local_ids[:, None] == vocab_index[None, :]).astype(jnp.bfloat16)
    own_rows = lax.psum_scatter(
        jnp.dot(onehot, embedding, preferred_element_type=jnp.float32),
        "fsdp",
        scatter_dimension=0,
        tiled=True,
    )
    features = lax.all_gather(own_rows.astype(jnp.bfloat16), "tp", axis=1, tiled=True)
    widened = features.astype(jnp.float32)
    normed = (
        widened
        * lax.rsqrt(jnp.mean(widened * widened, axis=-1, keepdims=True) + norm_eps)
        * norm_gain.astype(jnp.float32)
    ).astype(jnp.bfloat16)
    key_cols = head_key.shape[1]
    key_projector = jnp.dot(
        normed,
        lax.all_gather(head_key, "fsdp", axis=0, tiled=True),
        preferred_element_type=jnp.float32,
    )
    value_projector = jnp.dot(
        normed,
        lax.all_gather(head_value, "fsdp", axis=0, tiled=True),
        preferred_element_type=jnp.float32,
    )
    rollouts = token_ids.shape[0]
    heads_dev = key_cols // HEAD_SIZE
    heads_of_key = key_projector.reshape(rollouts, 2, heads_dev, HEAD_SIZE)
    key_normed = (
        heads_of_key
        * lax.rsqrt(jnp.mean(heads_of_key * heads_of_key, axis=-1, keepdims=True) + norm_eps)
        * key_norm_gain.astype(jnp.float32)
    )
    positions = (cache_lengths[:, None] + jnp.arange(2, dtype=jnp.int32)[None, :]).astype(
        jnp.float32
    )
    new_keys = rotate(key_normed, positions[:, :, None]).astype(jnp.bfloat16)
    incoming_values = value_projector.reshape(rollouts, 2, heads_dev, HEAD_SIZE).astype(
        jnp.bfloat16
    )
    head_groups = queries.shape[2] // key_cols
    slots = key_cache.shape[2]
    score_scale = HEAD_SIZE ** (-0.5)
    heads_of_query = queries.reshape(rollouts, 2, heads_dev, head_groups, HEAD_SIZE)
    cache_scores = (
        jnp.einsum(
            "rskgd,rkcd->rskgc", heads_of_query, key_cache, preferred_element_type=jnp.float32
        )
        * score_scale
    )
    valid_cache = jnp.arange(slots, dtype=jnp.int32)[None, :] < cache_lengths[:, None]
    cache_scores = jnp.where(valid_cache[:, None, None, None, :], cache_scores, -jnp.inf)
    fresh_scores = (
        jnp.einsum(
            "rskgd,rtkd->rskgt", heads_of_query, new_keys, preferred_element_type=jnp.float32
        )
        * score_scale
    )
    causal = jnp.arange(2)[None, :] <= jnp.arange(2)[:, None]
    fresh_scores = jnp.where(causal[None, :, None, None, :], fresh_scores, -jnp.inf)
    highest = jnp.maximum(jnp.max(cache_scores, axis=-1), jnp.max(fresh_scores, axis=-1))
    cache_exp = jnp.exp(cache_scores - highest[..., None])
    fresh_exp = jnp.exp(fresh_scores - highest[..., None])
    denominator = jnp.sum(cache_exp, axis=-1) + jnp.sum(fresh_exp, axis=-1)
    cache_share = (cache_exp / denominator[..., None]).astype(jnp.bfloat16)
    fresh_share = (fresh_exp / denominator[..., None]).astype(jnp.bfloat16)
    mixed = jnp.einsum(
        "rskgc,rkcd->rskgd", cache_share, cached_value_rows, preferred_element_type=jnp.float32
    )
    mixed = mixed + jnp.einsum(
        "rskgt,rtkd->rskgd", fresh_share, incoming_values, preferred_element_type=jnp.float32
    )
    attention = mixed.reshape(rollouts, 2, queries.shape[2]).astype(jnp.bfloat16)
    return (
        attention,
        new_key_weight,
        new_key_first,
        new_key_second,
        new_value_weight,
        new_value_first,
        new_value_second,
    )


def solution(mesh):
    placed = (
        P("fsdp", None),
        P("fsdp"),
        P("fsdp", "tp"),
        P(),
        P(),
        P(("fsdp", "tp"), None),
        P(("fsdp", "tp"), None),
        P(("fsdp", "tp"), None),
        P(("fsdp", "tp"), None),
        P(("fsdp", "tp"), None),
        P(("fsdp", "tp"), None),
        P(("fsdp", "tp"), None),
        P(("fsdp", "tp"), None),
        P("fsdp", None, "tp"),
        P("fsdp", "tp", None, None),
        P("fsdp", "tp", None, None),
    )
    return jax.shard_map(
        body,
        mesh=mesh,
        in_specs=placed,
        out_specs=(
            P("fsdp", None, "tp"),
            P(("fsdp", "tp"), None),
            P(("fsdp", "tp"), None),
            P(("fsdp", "tp"), None),
            P(("fsdp", "tp"), None),
            P(("fsdp", "tp"), None),
            P(("fsdp", "tp"), None),
        ),
        check_vma=False,
    )
```

profile of v0, /device:TPU:1, one launch (start us, length us, event | category | flops | bytes accessed | tf_op | source)
XLA Modules:
  0.0 554.5 jit_solution(4018441020397861936)
XLA Ops:
  7.2 0.0 copy-start
  7.2 2.0 fusion.37
  9.2 0.6 copy.40
  9.8 5.9 %all-to-all-start = ((bf16[10,8,128]{2,0,1:T(8,128)(2,1)}), bf16[10,8,128]{2,0,1:T(8,128)(2,1)S(1)}, u32[]{:S(2)}, u32[]{:S(2)}) async-start(bf16[10,8,128]{2,0,1:T(8,128)(2,1)} %copy.40), calls=%async_computation | async-start | bytes 65536 | tf_op jit(solution)/shard_map/all_to_all | solution.py:68
  15.7 84.0 %all-gather = s32[64,4,2]{1,2,0:T(2,128)S(1)} all-gather(s32[1,4,2]{1,2,0:T(2,128)} %bitcast.90), channel_id=1, replica_groups=mesh['fsdp'=64,'tp'=8] {'fsdp'}, dimensions={0}, use_global_device_ids=true | all-gather | bytes 2080 | tf_op jit(solution)/shard_map/all_gather | solution.py:76
  99.7 0.1 copy.38
  99.8 0.6 copy.42
  100.4 0.0 all-to-all-done
  100.4 4.8 all-to-all-start.1
  105.3 0.0 all-gather.4.cloned.1.call-start
  105.3 0.6 all_to_all.31
  105.9 0.1 all-gather.4.cloned.1.call-update
  106.0 0.0 all-gather.6.cloned.1.call-start
  106.1 0.1 copy.39
  106.2 0.2 sub.40
  106.4 0.0 copy-done
  106.4 1.3 fusion
  107.7 0.0 copy-start.3
  107.7 0.0 copy-start.2
  107.7 0.0 copy-start.4
  107.7 0.0 copy-start.1
  107.7 1.3 dynamic-slice
  109.6 264.9 %all-reduce.2 = bf16[512,640]{1,0:T(8,128)(2,1)} all-reduce(f32[512,640]{1,0:T(8,128)S(1)} %fusion), channel_id=2, replica_groups=mesh['fsdp'=64,'tp'=8] {'fsdp'}, use_global_device_ids=true, to_apply=%region_1.0.clone | all-reduce | flops 327680 | bytes 1966080
  374.5 0.7 dynamic-slice_convert_fusion
  375.2 22.4 %all_gather.13 = bf16[8,5120]{1,0:T(8,128)(2,1)S(1)} all-gather(bf16[8,640]{1,0:T(8,128)(2,1)S(1)} %dynamic-slice_convert_fusion), channel_id=1, replica_groups=mesh['fsdp'=64,'tp'=8] {'tp'}, dimensions={1}, use_global_device_ids=true | all-gather | bytes 92160 | tf_op jit(solution)/shard_map/all_gather | solution.py:86
  397.6 0.2 fusion.10
  397.8 0.0 copy-done.3
  397.8 0.1 add_convert_fusion
  397.9 0.0 copy-done.2
  397.9 0.0 all-to-all-done.1
  397.9 0.6 all_to_all.35
  398.6 0.0 all-gather.6.cloned.1.call-update
  398.6 0.1 iota_compare_fusion.2
  398.7 1.7 fusion.41
  400.4 1.8 multiply_reduce_fusion
  402.1 0.1 rsqrt.21
  402.2 0.1 multiply_multiply_fusion.2
  402.3 0.2 fusion.33
  402.5 0.2 convolution_multiply_fusion.1
  402.7 0.1 fusion.36
  402.8 0.1 fusion.20
  402.9 0.2 fusion.9
  403.1 0.1 fusion.30
  403.2 1.5 convolution_bitcast_fusion
  404.7 140.4 %all-gather.6.cloned.1.call-done = bf16[5120,128]{1,0:T(8,128)(2,1)} async-done(((bf16[80,128]{1,0:T(8,128)(2,1)}), bf16[5120,128]{1,0:T(8,128)(2,1)}) %all-gather.6.cloned.1.call-update) | async-done | bytes 1310736 | tf_op jit(solution)/shard_map/all_gather | solution.py:101
  545.2 1.6 convolution_convert_fusion
  546.8 0.2 fusion.6
  547.0 0.6 convert_element_type.75
  (17 shorter events, 0.1 us)
Async XLA Ops:
  7.2 99.2 %copy-start = (bf16[1280,640]{1,0:T(8,128)(2,1)S(1)}, bf16[1280,640]{1,0:T(8,128)(2,1)}, u32[]{:S(2)}) copy-start(bf16[1280,640]{1,0:T(8,128)(2,1)} %param.18) | copy-start | bytes 4915204
  9.8 90.7 %all-to-all-start = ((bf16[10,8,128]{2,0,1:T(8,128)(2,1)}), bf16[10,8,128]{2,0,1:T(8,128)(2,1)S(1)}, u32[]{:S(2)}, u32[]{:S(2)}) async-start(bf16[10,8,128]{2,0,1:T(8,128)(2,1)} %copy.40), calls=%async_computation | async-start | bytes 65536 | tf_op jit(solution)/shard_map/all_to_all | solution.py:68
  100.4 297.5 %all-to-all-start.1 = ((bf16[10,8,128]{2,0,1:T(8,128)(2,1)}), bf16[10,8,128]{2,0,1:T(8,128)(2,1)S(1)}, u32[]{:S(2)}, u32[]{:S(2)}) async-start(bf16[10,8,128]{2,0,1:T(8,128)(2,1)} %copy.42), calls=%async_computation.1 | async-start | bytes 65536 | tf_op jit(solution)/shard_map/all_to_all | solution.py:71
  105.3 295.1 %all-gather.4.cloned.1.call-start = ((), (), s32[]{:S(2)}) async-start(), calls=%async_computation.2 | async-start | bytes 1331200 | tf_op jit(solution)/shard_map/all_gather | solution.py:96
  106.0 439.2 %all-gather.6.cloned.1.call-start = ((), (), s32[]{:S(2)}) async-start(), calls=%async_computation.3 | async-start | bytes 1331200 | tf_op jit(solution)/shard_map/all_gather | solution.py:101
  107.7 290.1 %copy-start.3 = (s32[4]{0:T(128)S(1)}, s32[4]{0:T(128)}, u32[]{:S(2)}) copy-start(s32[4]{0:T(128)} %param.17) | copy-start | bytes 52
  107.7 290.2 %copy-start.2 = (bf16[5120]{0:T(1024)(128)(2,1)S(1)}, bf16[5120]{0:T(1024)(128)(2,1)}, u32[]{:S(2)}) copy-start(bf16[5120]{0:T(1024)(128)(2,1)} %param.19) | copy-start | bytes 30724
  107.7 290.2 %copy-start.4 = (bf16[128]{0:T(256)(128)(2,1)S(1)}, bf16[128]{0:T(256)(128)(2,1)}, u32[]{:S(2)}) copy-start(bf16[128]{0:T(256)(128)(2,1)} %param.20) | copy-start | bytes 772
  107.7 290.2 %copy-start.1 = (bf16[4,2,1024]{2,1,0:T(2,128)(2,1)S(1)}, bf16[4,2,1024]{2,1,0:T(2,128)(2,1)}, u32[]{:S(2)}) copy-start(bf16[4,2,1024]{2,1,0:T(2,128)(2,1)} %param.29) | copy-start | bytes 49156
Sparse Core Ops, SparseCore 0:
  109.3 136.1 all-gather.3
  398.7 146.4 all-gather.5
where the time goes:
time: 555 us; the launch traced here: 554 us
  blocking collectives  371 us (67%)
  waiting for transfers between devices  141 us (25%)
  between operations  14.9 us (3%)
  starting transfers between devices  10.8 us (2%)
  matrix products  8.32 us (1%)
  local copies, waits for them, and re-layouts  5.58 us (1%)
    unnamed x1, blocking collectives  265 us
    all_gather x1, waiting for transfers between devices, body(): lax.all_gather(head_value, 'fsdp', axis=0, tiled=True)  140 us
    all_gather x1, blocking collectives, body(): all_ids = lax.all_gather(token_ids, 'fsdp', axis=0, tiled=True).reshape(-1)  84 us
    all_gather x1, blocking collectives, body(): lax.all_gather(own_rows.astype(jnp.bfloat16), 'tp', axis=1, tiled=True)  22.4 us
  transfers between devices with their start and end apart: 4, of which 1 were waited for; matrix products, arithmetic and copies ran while one was open for 2% of the time, Pallas kernels for 0%

commit v1 on v0

v1 whole, which is shorter than its diff:
```python
import jax
import jax.numpy as jnp
from jax import lax
from jax.sharding import Mesh, PartitionSpec as P

HEAD_SIZE = 128


beta_one = 0.9
beta_two = 0.95
learn_rate = 0.001
weight_decay = 0.1
adam_eps = 1e-08
norm_eps = 1e-06
rope_base = 1000000.0


def adamw(weight, gradient, moment_one, moment_two):
    first_new = beta_one * moment_one + (1.0 - beta_one) * gradient
    second_new = beta_two * moment_two + (1.0 - beta_two) * gradient * gradient
    correct_one = 1.0 - beta_one**50
    correct_two = 1.0 - beta_two**50
    update = (
        first_new / correct_one / (jnp.sqrt(second_new / correct_two) + adam_eps)
        + weight_decay * weight
    )
    return (weight - learn_rate * update, first_new, second_new)


def rotate(vectors, positions):
    half_width = vectors.shape[-1] // 2
    frequency = rope_base ** (-jnp.arange(half_width, dtype=jnp.float32) * 2.0 / vectors.shape[-1])
    angles = positions[..., None] * frequency
    cosine = jnp.cos(angles)
    sine = jnp.sin(angles)
    upper_half = vectors[..., :half_width]
    lower_half = vectors[..., half_width:]
    return jnp.concatenate(
        [upper_half * cosine - lower_half * sine, lower_half * cosine + upper_half * sine], axis=-1
    )


def body(
    token_ids,
    cache_lengths,
    embedding,
    norm_gain,
    key_norm_gain,
    key_weight,
    key_grad,
    key_first,
    key_second,
    value_weight,
    value_grad,
    value_first,
    value_second,
    queries,
    key_cache,
    cached_value_rows,
):
    rollouts = token_ids.shape[0]
    tokens = 2 * rollouts
    z_size, quad_size, tp_size = lax.axis_size(Z), lax.axis_size(QUAD), lax.axis_size(TP)
    fsdp_size = z_size * quad_size

    own_ids = jnp.broadcast_to(token_ids.reshape(1, tokens), (fsdp_size, tokens))
    all_ids = lax.all_to_all(own_ids, FSDP, split_axis=0, concat_axis=0, tiled=False)

    new_key_weight, new_key_first, new_key_second = adamw(
        key_weight, key_grad, key_first, key_second
    )
    new_value_weight, new_value_first, new_value_second = adamw(
        value_weight, value_grad, value_first, value_second
    )
    own_rows = key_weight.shape[0]
    both = jnp.stack(
        [
            new_key_weight.astype(jnp.bfloat16).reshape(own_rows, tp_size, HEAD_SIZE),
            new_value_weight.astype(jnp.bfloat16).reshape(own_rows, tp_size, HEAD_SIZE),
        ],
        axis=2,
    ).reshape(own_rows, tp_size, 2 * HEAD_SIZE)
    head_rows = lax.all_to_all(
        both.transpose(1, 0, 2), TP, split_axis=0, concat_axis=0, tiled=False
    ).reshape(tp_size * own_rows, 2 * HEAD_SIZE)
    quad_rows = lax.all_gather(head_rows, QUAD, axis=0, tiled=True)
    projections = lax.all_gather(quad_rows, Z, axis=0, tiled=True)

    vocab_rows, features = embedding.shape
    ordered = all_ids.reshape(z_size, quad_size, tokens).transpose(1, 0, 2).reshape(-1)
    local_ids = ordered - lax.axis_index(FSDP) * vocab_rows
    vocab_index = jnp.arange(vocab_rows, dtype=jnp.int32)
    onehot = (local_ids[:, None] == vocab_index[None, :]).astype(jnp.bfloat16)
    found = jnp.dot(onehot, embedding, preferred_element_type=jnp.float32).astype(jnp.bfloat16)
    found = found.reshape(quad_size, z_size * tokens, features)
    found = lax.all_to_all(found, QUAD, split_axis=0, concat_axis=0, tiled=False)
    found = jnp.sum(found.astype(jnp.float32), axis=0).astype(jnp.bfloat16)
    found = found.reshape(z_size, tokens, features)
    found = lax.all_to_all(found, Z, split_axis=0, concat_axis=0, tiled=False)
    found = jnp.sum(found.astype(jnp.float32), axis=0).astype(jnp.bfloat16)
    found = jnp.broadcast_to(found[None], (tp_size, tokens, features))
    found = lax.all_to_all(found, TP, split_axis=0, concat_axis=0, tiled=False)
    embedded = found.transpose(1, 0, 2).reshape(tokens, tp_size * features)

    widened = embedded.astype(jnp.float32)
    normed = (
        widened
        * lax.rsqrt(jnp.mean(widened * widened, axis=-1, keepdims=True) + norm_eps)
        * norm_gain.astype(jnp.float32)
    ).astype(jnp.bfloat16)
    projected = jnp.dot(normed, projections, preferred_element_type=jnp.float32)
    heads_of_key = projected[:, :HEAD_SIZE].reshape(rollouts, 2, HEAD_SIZE)
    key_normed = (
        heads_of_key
        * lax.rsqrt(jnp.mean(heads_of_key * heads_of_key, axis=-1, keepdims=True) + norm_eps)
        * key_norm_gain.astype(jnp.float32)
    )
    positions = (cache_lengths[:, None] + jnp.arange(2, dtype=jnp.int32)[None, :]).astype(
        jnp.float32
    )
    new_keys = rotate(key_normed, positions).astype(jnp.bfloat16)
    new_values = projected[:, HEAD_SIZE:].reshape(rollouts, 2, HEAD_SIZE).astype(jnp.bfloat16)

    groups = queries.shape[2] // HEAD_SIZE
    slots = key_cache.shape[2]
    score_scale = HEAD_SIZE ** (-0.5)
    rows = queries.reshape(rollouts, 2 * groups, HEAD_SIZE)
    cache_scores = (
        jnp.einsum("rqd,rcd->rqc", rows, key_cache[:, 0], preferred_element_type=jnp.float32)
        * score_scale
    )
    valid_cache = jnp.arange(slots, dtype=jnp.int32)[None, :] < cache_lengths[:, None]
    cache_scores = jnp.where(valid_cache[:, None, :], cache_scores, -jnp.inf)
    cache_highest = jnp.max(cache_scores, axis=-1, keepdims=True)
    cache_exp = jnp.exp(cache_scores - cache_highest)
    cache_sum = jnp.sum(cache_exp, axis=-1, keepdims=True)
    cache_mixed = jnp.einsum(
        "rqc,rcd->rqd",
        cache_exp.astype(jnp.bfloat16),
        cached_value_rows[:, 0],
        preferred_element_type=jnp.float32,
    )

    fresh_scores = (
        jnp.einsum("rqd,rtd->rqt", rows, new_keys, preferred_element_type=jnp.float32)
        * score_scale
    )
    step = jnp.arange(2 * groups) // groups
    causal = jnp.arange(2)[None, :] <= step[:, None]
    fresh_scores = jnp.where(causal[None], fresh_scores, -jnp.inf)
    highest = jnp.maximum(cache_highest, jnp.max(fresh_scores, axis=-1, keepdims=True))
    cache_factor = jnp.exp(cache_highest - highest)
    fresh_exp = jnp.exp(fresh_scores - highest)
    denominator = cache_sum * cache_factor + jnp.sum(fresh_exp, axis=-1, keepdims=True)
    mixed = cache_mixed * cache_factor + jnp.einsum(
        "rqt,rtd->rqd",
        fresh_exp.astype(jnp.bfloat16),
        new_values,
        preferred_element_type=jnp.float32,
    )
    attention = (mixed / denominator).reshape(rollouts, 2, queries.shape[2]).astype(jnp.bfloat16)
    return (
        attention,
        new_key_weight,
        new_key_first,
        new_key_second,
        new_value_weight,
        new_value_first,
        new_value_second,
    )


Z = "z"
QUAD = ("xh", "core")
FSDP = ("z", "xh", "core")
TP = "tp"


def solution(mesh):
    fine = Mesh(mesh.devices.reshape(16, 2, 2, 8), ("z", "xh", "core", "tp"))
    rows = P(FSDP + (TP,), None)
    placed = (
        P(FSDP, None),
        P(FSDP),
        P(FSDP, TP),
        P(),
        P(),
        *[rows] * 8,
        P(FSDP, None, TP),
        P(FSDP, TP, None, None),
        P(FSDP, TP, None, None),
    )
    return jax.shard_map(
        body,
        mesh=fine,
        in_specs=placed,
        out_specs=(P(FSDP, None, TP), *[rows] * 6),
        check_vma=False,
    )
```

time: 555 us -> 126 us (0.23)
  the two profiles are of different devices: /device:TPU:1 before, /device:TPU:2 now
where the time goes in v1:
time: 126 us; the launch traced here: 125 us
  waiting for transfers between devices  46.6 us (37%)
  starting transfers between devices  28.5 us (23%)
  blocking collectives  20.8 us (17%)
  between operations  14.3 us (11%)
  matrix products  6.77 us (5%)
  other arithmetic  5.12 us (4%)
  local copies, waits for them, and re-layouts  3.04 us (2%)
    all_to_all x1, waiting for transfers between devices, body(): found = lax.all_to_all(found, Z, split_axis=0, concat_axis=0, tiled=False)  16.5 us
    all_to_all x1, starting transfers between devices, body(): lax.all_to_all(own_ids, FSDP, split_axis=0, concat_axis=0, tiled=False)  15.1 us
    all_to_all x1, waiting for transfers between devices, body(): lax.all_to_all(own_ids, FSDP, split_axis=0, concat_axis=0, tiled=False)  15 us
    all_to_all x1, blocking collectives, body(): lax.all_to_all(both.transpose(1, 0, 2), TP, split_axis=0, concat_axis=0,...  13.3 us
    all_to_all x1, waiting for transfers between devices, body(): lax.all_to_all(found, QUAD, split_axis=0, concat_axis=0, tiled=False)  9.9 us
    all_gather x1, blocking collectives, body(): quad_rows = lax.all_gather(head_rows, QUAD, axis=0, tiled=True)  7.47 us
    all_to_all x1, starting transfers between devices, body(): found = lax.all_to_all(found, TP, split_axis=0, concat_axis=0, tiled=False)  6.08 us
    all_to_all x1, waiting for transfers between devices, body(): found = lax.all_to_all(found, TP, split_axis=0, concat_axis=0, tiled=False)  5.17 us
  transfers between devices with their start and end apart: 5, of which 4 were waited for; matrix products, arithmetic and copies ran while one was open for 6% of the time, Pallas kernels for 0%

profile of v1, /device:TPU:2, one launch (start us, length us, event | category | flops | bytes accessed | tf_op | source)
XLA Modules:
  0.0 125.1 jit_solution(8821946638919441544)
XLA Ops:
  7.2 0.0 copy-start
  7.2 0.0 all-gather.2.cloned.1.call-start
  7.2 1.7 %fusion.35 = (bf16[10,1024]{1,0:T(8,128)(2,1)S(1)}, f32[10,1024]{1,0:T(8,128)}, f32[10,1024]{1,0:T(8,128)}, f32[10,1024]{1,0:T(8,128)}) fusion(f32[10,1024]{1,0:T(8,128)} %param.21, f32[10,1024]{1,0:T(8,128)} %param.22, f32[10,1024]{1,0:T(8,128)} %param.23, f32[10,1024]{1,0:T(8,128)} %param.24), kind=kLoop, calls=%fused_computation.69 | loop fusion | flops 163840 | bytes 307200 | tf_op jit(solution)/shard_map/convert_element_type | solution.py:78
  9.0 1.6 %fusion.37 = (bf16[10,1024]{1,0:T(8,128)(2,1)S(1)}, f32[10,1024]{1,0:T(8,128)}, f32[10,1024]{1,0:T(8,128)}, f32[10,1024]{1,0:T(8,128)}) fusion(f32[10,1024]{1,0:T(8,128)} %param.25, f32[10,1024]{1,0:T(8,128)} %param.26, f32[10,1024]{1,0:T(8,128)} %param.27, f32[10,1024]{1,0:T(8,128)} %param.28), kind=kLoop, calls=%fused_computation.70 | loop fusion | flops 163840 | bytes 307200 | tf_op jit(solution)/shard_map/convert_element_type | solution.py:79
  10.7 13.3 %all_to_all.26 = bf16[8,10,256]{2,1,0:T(8,128)(2,1)S(1)} all-to-all(bf16[8,10,256]{2,1,0:T(8,128)(2,1)S(1)} %copy.34), channel_id=1, replica_groups=mesh['z'=16,'xh'=2,'core'=2,'tp'=8] {'tp'}, dimensions={0} | all-to-all | bytes 81920 | tf_op jit(solution)/shard_map/all_to_all | solution.py:83
  24.1 7.5 %all_gather.6 = bf16[320,256]{1,0:T(8,128)(2,1)} all-gather(bf16[80,256]{1,0:T(8,128)(2,1)S(1)} %reshape.194), channel_id=1, replica_groups=mesh['z'=16,'xh'=2,'core'=2,'tp'=8] {'xh','core'}, dimensions={0}, use_global_device_ids=true | all-gather | bytes 204800 | tf_op jit(solution)/shard_map/all_gather | solution.py:86
  31.5 0.0 all-gather.2.cloned.1.call-update
  31.5 0.8 copy.32
  32.3 0.1 broadcast_in_dim.29
  32.4 0.6 broadcast_in_dim.30
  33.0 15.1 %all-to-all-start = ((s32[64,1,8]{2,1,0:T(1,128)}), s32[64,1,8]{2,1,0:T(1,128)S(1)}, u32[]{:S(2)}, u32[]{:S(2)}) async-start(s32[64,1,8]{2,1,0:T(1,128)} %broadcast_in_dim.30), calls=%async_computation | async-start | bytes 65536 | tf_op jit(solution)/shard_map/all_to_all | solution.py:67
  48.1 15.0 %all-to-all-done = s32[64,1,8]{2,1,0:T(1,128)S(1)} async-done(((s32[64,1,8]{2,1,0:T(1,128)}), s32[64,1,8]{2,1,0:T(1,128)S(1)}, u32[]{:S(2)}, u32[]{:S(2)}) %all-to-all-start) | async-done | bytes 2080 | tf_op jit(solution)/shard_map/all_to_all | solution.py:67
  63.2 0.1 sub.66
  63.3 0.0 copy-done
  63.3 0.0 copy-start.2
  63.3 0.0 copy-start.4
  63.3 2.1 %fusion.1 = bf16[512,640]{1,0:T(8,128)(2,1)} fusion(bf16[1280,640]{1,0:T(8,128)(2,1)S(1)} %copy-done, s32[512]{0:T(512)S(1)} %sub.66), kind=kOutput, calls=%fused_computation.2 | convolution fusion | flops 839843840 | bytes 2295808 | tf_op jit(solution)/shard_map/dot_general | solution.py:94
  65.4 0.0 copy-start.3
  65.4 0.0 copy-start.5
  65.4 3.6 %all-to-all-start.1 = ((bf16[4,128,640]{2,1,0:T(8,128)(2,1)}), bf16[4,128,640]{2,1,0:T(8,128)(2,1)S(1)}, u32[]{:S(2)}, u32[]{:S(2)}) async-start(bf16[4,128,640]{2,1,0:T(8,128)(2,1)} %bitcast.4), calls=%async_computation.1 | async-start | bytes 1310720 | tf_op jit(solution)/shard_map/all_to_all | solution.py:96
  69.0 0.0 copy-done.2
  69.1 0.0 copy-done.4
  69.1 0.1 iota_compare_fusion.4
  69.2 1.7 %fusion.39 = (f32[4,16]{1,0:T(4,128)S(1)}, f32[4,16,1024]{2,1,0:T(8,128)S(1)}) fusion(bf16[4,16,128]{2,1,0:T(8,128)(2,1)S(1)} %reshape.190, bf16[4,1,1024,128]{3,2,1,0:T(8,128)(2,1)} %param.30, pred[4,1024]{1,0:T(4,128)(4,1)S(1)} %iota_compare_fusion.4), kind=kOutput, calls=%fused_computation.71 | convolution fusion | flops 16973760 | bytes 1331456 | tf_op jit(solution)/shard_map/rqd,rcd->rqc/dot_general | solution.py:129
  70.9 9.9 %all-to-all-done.1 = bf16[4,128,640]{2,1,0:T(8,128)(2,1)S(1)} async-done(((bf16[4,128,640]{2,1,0:T(8,128)(2,1)}), bf16[4,128,640]{2,1,0:T(8,128)(2,1)S(1)}, u32[]{:S(2)}, u32[]{:S(2)}) %all-to-all-start.1) | async-done | bytes 655392 | tf_op jit(solution)/shard_map/all_to_all | solution.py:96
  80.8 0.8 reduce_sum.60
  81.5 0.0 copy-start.1
  81.5 3.6 %all-to-all-start.2 = ((bf16[16,8,640]{2,1,0:T(8,128)(2,1)}), bf16[16,8,640]{2,1,0:T(8,128)(2,1)S(1)}, u32[]{:S(2)}, u32[]{:S(2)}) async-start(bf16[16,8,640]{2,1,0:T(8,128)(2,1)} %bitcast.5), calls=%async_computation.2 | async-start | bytes 327680 | tf_op jit(solution)/shard_map/all_to_all | solution.py:99
  85.2 0.0 copy-done.3
  85.2 0.0 copy-done.5
  85.3 0.2 fusion.10
  85.5 0.1 add_convert_fusion
  85.5 16.5 %all-to-all-done.2 = bf16[16,8,640]{2,1,0:T(8,128)(2,1)S(1)} async-done(((bf16[16,8,640]{2,1,0:T(8,128)(2,1)}), bf16[16,8,640]{2,1,0:T(8,128)(2,1)S(1)}, u32[]{:S(2)}, u32[]{:S(2)}) %all-to-all-start.2) | async-done | bytes 163872 | tf_op jit(solution)/shard_map/all_to_all | solution.py:99
  102.0 0.6 broadcast_in_dim.31
  102.7 6.1 %all-to-all-start.3 = ((bf16[8,8,640]{2,1,0:T(8,128)(2,1)}), bf16[8,8,640]{2,1,0:T(8,128)(2,1)S(1)}, u32[]{:S(2)}, u32[]{:S(2)}) async-start(bf16[8,8,640]{2,1,0:T(8,128)(2,1)} %broadcast_in_dim.31), calls=%async_computation.3 | async-start | bytes 163840 | tf_op jit(solution)/shard_map/all_to_all | solution.py:102
  108.8 5.2 %all-to-all-done.3 = bf16[8,8,640]{2,1,0:T(8,128)(2,1)S(1)} async-done(((bf16[8,8,640]{2,1,0:T(8,128)(2,1)}), bf16[8,8,640]{2,1,0:T(8,128)(2,1)S(1)}, u32[]{:S(2)}, u32[]{:S(2)}) %all-to-all-start.3) | async-done | bytes 81952 | tf_op jit(solution)/shard_map/all_to_all | solution.py:102
  113.9 0.2 multiply_reduce_fusion
  114.1 0.0 all-gather.2.cloned.1.call-done
  114.1 2.2 %fusion.14 = f32[8,256]{1,0:T(8,128)S(1)} fusion(bf16[5120,256]{1,0:T(8,128)(2,1)} %all-gather.2.cloned.1.call-done, f32[8,5120]{1,0:T(8,128)S(1)} %bitcast.45, f32[5120]{0:T(1024)S(1)} %convert_element_type.66, f32[8]{0:T(128)S(1)} %add_rsqrt_fusion.1), kind=kOutput, calls=%fused_computation.23 | convolution fusion | flops 21094400 | bytes 2813984 | tf_op jit(solution)/shard_map/dot_general | solution.py:111
  116.4 0.1 multiply_reduce_fusion.1
  116.5 0.1 rsqrt.21
  116.6 0.1 multiply_multiply_fusion.2
  116.7 0.1 fusion.26
  116.8 0.2 fusion.40
  117.1 0.0 copy-done.1
  117.1 0.3 convolution_multiply_fusion.1
  117.4 0.2 fusion.5
  117.6 0.6 convert_element_type.75
  (22 shorter events, 0.2 us)
Async XLA Ops:
  7.2 56.1 %copy-start = (bf16[1280,640]{1,0:T(8,128)(2,1)S(1)}, bf16[1280,640]{1,0:T(8,128)(2,1)}, u32[]{:S(2)}) copy-start(bf16[1280,640]{1,0:T(8,128)(2,1)} %param.18) | copy-start | bytes 4915204
  7.2 106.9 %all-gather.2.cloned.1.call-start = ((), (), s32[]{:S(2)}) async-start(), calls=%async_computation.5 | async-start | bytes 2785280 | tf_op jit(solution)/shard_map/all_gather | solution.py:87
  33.0 30.1 %all-to-all-start = ((s32[64,1,8]{2,1,0:T(1,128)}), s32[64,1,8]{2,1,0:T(1,128)S(1)}, u32[]{:S(2)}, u32[]{:S(2)}) async-start(s32[64,1,8]{2,1,0:T(1,128)} %broadcast_in_dim.30), calls=%async_computation | async-start | bytes 65536 | tf_op jit(solution)/shard_map/all_to_all | solution.py:67
  63.3 5.8 %copy-start.2 = (bf16[4,2,1024]{2,1,0:T(2,128)(2,1)S(1)}, bf16[4,2,1024]{2,1,0:T(2,128)(2,1)}, u32[]{:S(2)}) copy-start(bf16[4,2,1024]{2,1,0:T(2,128)(2,1)} %param.29) | copy-start | bytes 49156
  63.3 5.8 %copy-start.4 = (s32[4]{0:T(128)S(1)}, s32[4]{0:T(128)}, u32[]{:S(2)}) copy-start(s32[4]{0:T(128)} %param.17) | copy-start | bytes 52
  65.4 19.8 %copy-start.3 = (bf16[5120]{0:T(1024)(128)(2,1)S(1)}, bf16[5120]{0:T(1024)(128)(2,1)}, u32[]{:S(2)}) copy-start(bf16[5120]{0:T(1024)(128)(2,1)} %param.19) | copy-start | bytes 30724
  65.4 19.8 %copy-start.5 = (bf16[128]{0:T(256)(128)(2,1)S(1)}, bf16[128]{0:T(256)(128)(2,1)}, u32[]{:S(2)}) copy-start(bf16[128]{0:T(256)(128)(2,1)} %param.20) | copy-start | bytes 772
  65.4 15.3 %all-to-all-start.1 = ((bf16[4,128,640]{2,1,0:T(8,128)(2,1)}), bf16[4,128,640]{2,1,0:T(8,128)(2,1)S(1)}, u32[]{:S(2)}, u32[]{:S(2)}) async-start(bf16[4,128,640]{2,1,0:T(8,128)(2,1)} %bitcast.4), calls=%async_computation.1 | async-start | bytes 1310720 | tf_op jit(solution)/shard_map/all_to_all | solution.py:96
  81.5 35.5 %copy-start.1 = (bf16[4,1,1024,128]{3,2,1,0:T(8,128)(2,1)S(1)}, bf16[4,1,1024,128]{3,2,1,0:T(8,128)(2,1)}, u32[]{:S(2)}) copy-start(bf16[4,1,1024,128]{3,2,1,0:T(8,128)(2,1)} %param.31) | copy-start | bytes 3145732
  81.5 20.4 %all-to-all-start.2 = ((bf16[16,8,640]{2,1,0:T(8,128)(2,1)}), bf16[16,8,640]{2,1,0:T(8,128)(2,1)S(1)}, u32[]{:S(2)}, u32[]{:S(2)}) async-start(bf16[16,8,640]{2,1,0:T(8,128)(2,1)} %bitcast.5), calls=%async_computation.2 | async-start | bytes 327680 | tf_op jit(solution)/shard_map/all_to_all | solution.py:99
  102.7 11.3 %all-to-all-start.3 = ((bf16[8,8,640]{2,1,0:T(8,128)(2,1)}), bf16[8,8,640]{2,1,0:T(8,128)(2,1)S(1)}, u32[]{:S(2)}, u32[]{:S(2)}) async-start(bf16[8,8,640]{2,1,0:T(8,128)(2,1)} %broadcast_in_dim.31), calls=%async_computation.3 | async-start | bytes 163840 | tf_op jit(solution)/shard_map/all_to_all | solution.py:102
Sparse Core Ops, SparseCore 0:
  31.7 80.9 all-gather.1

commit v2 on v1

v2 whole, which is shorter than its diff:
```python
import jax
import jax.numpy as jnp
from jax import lax
from jax.experimental import pallas as pl
from jax.experimental.pallas import tpu as pltpu
from jax.sharding import Mesh
from jax.sharding import PartitionSpec as P

HEAD_SIZE = 128
LANES = 128
BLOCK_ROWS = 40
BLOCK = 48
CHUNK = 384
HIGH_COLUMN = 40
LOW_COLUMN = 41


beta_one = 0.9
beta_two = 0.95
learn_rate = 0.001
weight_decay = 0.1
adam_eps = 1e-08
norm_eps = 1e-06
rope_base = 1000000.0


def adamw(weight, gradient, moment_one, moment_two):
    first_new = beta_one * moment_one + (1.0 - beta_one) * gradient
    second_new = beta_two * moment_two + (1.0 - beta_two) * gradient * gradient
    correct_one = 1.0 - beta_one**50
    correct_two = 1.0 - beta_two**50
    update = (
        first_new / correct_one / (jnp.sqrt(second_new / correct_two) + adam_eps)
        + weight_decay * weight
    )
    return (weight - learn_rate * update, first_new, second_new)


def call(kernel, shape, dtype, *operands):
    return pl.pallas_call(
        kernel,
        out_shape=jax.ShapeDtypeStruct(shape, dtype),
        compiler_params=pltpu.CompilerParams(vmem_limit_bytes=16 * 1024 * 1024),
    )(*operands)


def look_up(ids_ref, table_ref, other_ref, sort_ref, found_ref):
    count = ids_ref.shape[1]
    eye = lax.broadcasted_iota(jnp.int32, (count, count), 0) == lax.broadcasted_iota(
        jnp.int32, (count, count), 1
    )
    total = jnp.zeros((count, table_ref.shape[1]), jnp.float32)
    for part, held in enumerate((table_ref, other_ref)):
        row = jnp.broadcast_to(ids_ref[part : part + 1, :], (count, count))
        ids = jnp.sum(jnp.where(eye, row, 0), axis=1, keepdims=True)
        index = lax.broadcasted_iota(jnp.int32, (count, held.shape[0]), 1)
        onehot = jnp.where(ids == index, 1.0, 0.0).astype(jnp.bfloat16)
        total += jnp.dot(onehot, held[...], preferred_element_type=jnp.float32)
    found_ref[...] = jnp.dot(
        total.astype(jnp.bfloat16), sort_ref[...], preferred_element_type=jnp.float32
    ).astype(jnp.bfloat16)


def split_rows(came_ref, chunks_ref):
    total = came_ref[0].astype(jnp.float32) + came_ref[1].astype(jnp.float32)
    squares = jnp.sum(jnp.sum(total * total, axis=0), axis=-1, keepdims=True)
    high = squares.astype(jnp.bfloat16).astype(jnp.float32)
    low = squares - high
    column = lax.broadcasted_iota(jnp.int32, (squares.shape[0], CHUNK), 1)
    extra = jnp.where(column == HIGH_COLUMN, high, jnp.where(column == LOW_COLUMN, low, 0.0))
    for place in range(total.shape[0]):
        for half in range(2):
            chunk = total[place, :, half * CHUNK : (half + 1) * CHUNK] + extra
            chunks_ref[2 * place + half] = chunk.astype(jnp.bfloat16)


def pack(came_ref, weight_ref, packed_ref):
    rows = jnp.sum(came_ref[...].astype(jnp.float32), axis=0).astype(jnp.bfloat16)
    count = rows.shape[0]
    parts = CHUNK // LANES
    for place in range(packed_ref.shape[0]):
        for part in range(parts):
            packed_ref[place, part * count : (part + 1) * count, :] = rows[
                :, part * LANES : (part + 1) * LANES
            ]
        packed_ref[place, parts * count : parts * count + BLOCK, :] = weight_ref[place, :, :LANES]
        packed_ref[place, parts * count + BLOCK :, :] = weight_ref[place, :, LANES:]


def project(came_ref, gain_ref, product_ref):
    places = came_ref.shape[0]
    parts = CHUNK // LANES
    count = (came_ref.shape[1] - 2 * BLOCK) // parts
    rows = [
        came_ref[:, part * count : (part + 1) * count, :]
        .reshape(places * count, LANES)
        .astype(jnp.float32)
        for part in range(parts)
    ]
    column = lax.broadcasted_iota(jnp.int32, rows[0].shape, 1)
    marked = (column == HIGH_COLUMN) | (column == LOW_COLUMN)
    squares = jnp.sum(jnp.where(marked, rows[0], 0.0), axis=-1, keepdims=True)
    factor = lax.rsqrt(squares / FEATURES + norm_eps)
    normed = jnp.concatenate(
        [
            (rows[part] * factor * gain_ref[:, part * LANES : (part + 1) * LANES]).astype(
                jnp.bfloat16
            )
            for part in range(parts)
        ],
        axis=1,
    )
    for side in range(2):
        start = parts * count + side * BLOCK
        weight = came_ref[:, start : start + BLOCK, :].reshape(places * BLOCK, LANES)
        product = jnp.dot(normed, weight, preferred_element_type=jnp.float32)
        product_ref[:, :, side * LANES : (side + 1) * LANES] = product.reshape(
            product_ref.shape[0], product_ref.shape[1], LANES
        )


def finish(
    came_ref, gain_ref, cosine_ref, sine_ref, query_ref, mixed_ref, highest_ref, sum_ref, out_ref
):
    total = jnp.sum(came_ref[...], axis=0)
    keys = total[:, :LANES]
    values = total[:, LANES:].astype(jnp.bfloat16)
    factor = lax.rsqrt(jnp.mean(keys * keys, axis=-1, keepdims=True) + norm_eps)
    keys = keys * factor * gain_ref[...]
    turned = jnp.concatenate([keys[:, LANES // 2 :], keys[:, : LANES // 2]], axis=1)
    keys = (keys * cosine_ref[...] + turned * sine_ref[...]).astype(jnp.bfloat16)
    count = query_ref.shape[0]
    fresh = lax.dot_general(
        query_ref[...], keys, (((1,), (1,)), ((), ())), preferred_element_type=jnp.float32
    ) * (HEAD_SIZE**-0.5)
    row = lax.broadcasted_iota(jnp.int32, fresh.shape, 0)
    column = lax.broadcasted_iota(jnp.int32, fresh.shape, 1)
    each = count // (keys.shape[0] // 2)
    step = row % each // (each // 2)
    joined = (row // each == column // 2) & (column % 2 <= step)
    fresh = jnp.where(joined, fresh, -jnp.inf)
    highest = jnp.maximum(highest_ref[...], jnp.max(fresh, axis=-1, keepdims=True))
    weights = jnp.exp(fresh - highest)
    factor = jnp.exp(highest_ref[...] - highest)
    denominator = sum_ref[...] * factor + jnp.sum(weights, axis=-1, keepdims=True)
    mixed = mixed_ref[...] * factor + jnp.dot(
        weights,
        values.astype(jnp.float32),
        precision=lax.Precision.HIGHEST,
        preferred_element_type=jnp.float32,
    )
    mixed = (mixed / denominator).astype(jnp.bfloat16)
    groups = each // 2
    for at in range(2 * out_ref.shape[0]):
        for group in range(groups):
            out_ref[at // 2, at % 2 : at % 2 + 1, group * HEAD_SIZE : (group + 1) * HEAD_SIZE] = (
                mixed[at * groups + group : at * groups + group + 1, :]
            )


FEATURES = 5120


def body(
    token_ids,
    cache_lengths,
    embedding,
    norm_gain,
    key_norm_gain,
    key_weight,
    key_grad,
    key_first,
    key_second,
    value_weight,
    value_grad,
    value_first,
    value_second,
    queries,
    key_cache,
    cached_value_rows,
):
    rollouts = token_ids.shape[0]
    tokens = 2 * rollouts
    z_size, quad_size, tp_size = lax.axis_size("z"), lax.axis_size(QUAD), lax.axis_size(TP)
    own_rows = key_weight.shape[0]
    vocab_rows, features = embedding.shape

    chips = z_size * lax.axis_size("xh")
    own_ids = jnp.broadcast_to(token_ids.reshape(1, tokens), (chips, tokens))
    all_ids = lax.all_to_all(own_ids, ("xh", "z"), split_axis=0, concat_axis=0, tiled=False)

    column = jnp.arange(2 * CHUNK, dtype=jnp.int32)
    half, place = column // CHUNK, column % CHUNK // BLOCK
    row = column % BLOCK
    feature = half * (features // 2) + (row // own_rows * tp_size + place) * own_rows + row % own_rows
    feature = jnp.where(row < BLOCK_ROWS, feature, -1)
    sort = (jnp.arange(features, dtype=jnp.int32)[:, None] == feature[None, :]).astype(jnp.bfloat16)
    other_table = lax.ppermute(embedding, "core", [(0, 1), (1, 0)])

    new_key_weight, new_key_first, new_key_second = adamw(
        key_weight, key_grad, key_first, key_second
    )
    new_value_weight, new_value_first, new_value_second = adamw(
        value_weight, value_grad, value_first, value_second
    )
    both = jnp.stack(
        [
            new_key_weight.astype(jnp.bfloat16).reshape(own_rows, tp_size, HEAD_SIZE),
            new_value_weight.astype(jnp.bfloat16).reshape(own_rows, tp_size, HEAD_SIZE),
        ],
        axis=2,
    ).reshape(own_rows, 2 * tp_size * HEAD_SIZE)
    quad_rows = lax.all_gather(both, QUAD, axis=0, tiled=False)
    quad_rows = quad_rows.reshape(quad_size * own_rows, tp_size, 2 * HEAD_SIZE).transpose(1, 0, 2)
    quad_rows = jnp.pad(quad_rows, ((0, 0), (0, BLOCK - BLOCK_ROWS), (0, 0)))

    all_ids, quad_rows = lax.optimization_barrier((all_ids, quad_rows))

    gain = jnp.dot(
        norm_gain.reshape(z_size, -1), sort[: features // 2, :CHUNK], preferred_element_type=jnp.float32
    )
    gain = lax.dynamic_slice_in_dim(gain, lax.axis_index("z"), 1, axis=0)

    groups = queries.shape[2] // HEAD_SIZE
    slots = key_cache.shape[2]
    score_scale = HEAD_SIZE ** (-0.5)
    rows = queries.reshape(rollouts, 2 * groups, HEAD_SIZE)
    cache_scores = (
        jnp.einsum("rqd,rcd->rqc", rows, key_cache[:, 0], preferred_element_type=jnp.float32)
        * score_scale
    )
    valid_cache = jnp.arange(slots, dtype=jnp.int32)[None, :] < cache_lengths[:, None]
    cache_scores = jnp.where(valid_cache[:, None, :], cache_scores, -jnp.inf)
    cache_highest = jnp.max(cache_scores, axis=-1, keepdims=True)
    cache_exp = jnp.exp(cache_scores - cache_highest)
    cache_sum = jnp.sum(cache_exp, axis=-1, keepdims=True)
    high = cache_exp.astype(jnp.bfloat16)
    low = (cache_exp - high.astype(jnp.float32)).astype(jnp.bfloat16)
    cache_mixed = jnp.einsum(
        "rqc,rcd->rqd",
        jnp.concatenate([high, low], axis=1),
        cached_value_rows[:, 0],
        preferred_element_type=jnp.float32,
    )
    cache_mixed = cache_mixed[:, : 2 * groups] + cache_mixed[:, 2 * groups :]

    positions = (cache_lengths[:, None] + jnp.arange(2, dtype=jnp.int32)[None, :]).astype(
        jnp.float32
    )
    frequency = rope_base ** (
        -jnp.arange(HEAD_SIZE // 2, dtype=jnp.float32) * 2.0 / HEAD_SIZE
    )
    angles = positions.reshape(tokens, 1) * frequency
    cosine, sine = jnp.cos(angles), jnp.sin(angles)
    cosine = jnp.concatenate([cosine, cosine], axis=1)
    sine = jnp.concatenate([-sine, sine], axis=1)

    part = lax.axis_index(FSDP)
    owners = jnp.stack([part, part ^ 1])
    ids = all_ids.reshape(1, -1) - owners[:, None] * vocab_rows
    found = call(
        look_up, (ids.shape[1], 2 * CHUNK), jnp.bfloat16, ids, embedding, other_table, sort
    )
    each = 2 * tokens
    found = found.reshape(-1, each, 2 * CHUNK)
    found = lax.all_to_all(found, ("xh", TP), split_axis=0, concat_axis=0, tiled=False)
    found = found.reshape(2, tp_size, each, 2 * CHUNK)
    found = call(split_rows, (z_size, each, CHUNK), jnp.bfloat16, found)
    found = lax.all_to_all(found, "z", split_axis=0, concat_axis=0, tiled=False)
    message_rows = CHUNK // LANES * each + 2 * BLOCK
    packed = call(pack, (tp_size, message_rows, LANES), jnp.bfloat16, found, quad_rows)
    packed = lax.all_to_all(packed, TP, split_axis=0, concat_axis=0, tiled=False)
    product = call(project, (z_size, tokens, 2 * HEAD_SIZE), jnp.float32, packed, gain)
    product = lax.all_to_all(product, "z", split_axis=0, concat_axis=0, tiled=False)
    attention = call(
        finish,
        queries.shape,
        jnp.bfloat16,
        product,
        key_norm_gain.astype(jnp.float32).reshape(1, HEAD_SIZE),
        cosine,
        sine,
        rows.reshape(-1, HEAD_SIZE),
        cache_mixed.reshape(-1, HEAD_SIZE),
        cache_highest.reshape(-1, 1),
        cache_sum.reshape(-1, 1),
    )
    return (
        attention,
        new_key_weight,
        new_key_first,
        new_key_second,
        new_value_weight,
        new_value_first,
        new_value_second,
    )


QUAD = ("xh", "core")
FSDP = ("z", "xh", "core")
TP = "tp"


def solution(mesh):
    fine = Mesh(mesh.devices.reshape(16, 2, 2, 8), ("z", "xh", "core", "tp"))
    rows = P(FSDP + (TP,), None)
    placed = (
        P(FSDP, None),
        P(FSDP),
        P(FSDP, TP),
        P(),
        P(),
        *[rows] * 8,
        P(FSDP, None, TP),
        P(FSDP, TP, None, None),
        P(FSDP, TP, None, None),
    )
    return jax.shard_map(
        body,
        mesh=fine,
        in_specs=placed,
        out_specs=(P(FSDP, None, TP), *[rows] * 6),
        check_vma=False,
    )
```

time: 126 us -> 117 us (0.929)
  starting transfers between devices: 28.5 us -> 46.1 us
  between operations: 14.3 us -> 0.83 us
  blocking collectives: 20.8 us -> 7.59 us
  Pallas kernels: 0 us -> 7.8 us
  matrix products: 6.77 us -> 0.94 us
  waiting for transfers between devices: 46.6 us -> 45.3 us
  other arithmetic: 5.12 us -> 3.82 us
    all_to_all x4 -> x5, starting transfers between devices: 28.5 us -> 44 us  [the longest x1 17 us: body(): lax.all_to_all(own_ids, ('xh', 'z'), split_axis=0, concat_axis=0, tiled=F...]
    all_to_all x1 -> x0, blocking collectives: 13.3 us -> none  [body(): lax.all_to_all(both.transpose(1, 0, 2), TP, split_axis=0, concat_axis=0,...]
    pallas_call x0 -> x5, Pallas kernels: none -> 7.8 us  [call(): pl.pallas_call(kernel, out_shape=jax.ShapeDtypeStruct(shape, dtype), comp...]
    dot_general x5 -> x2, matrix products: 5.07 us -> 0.47 us  [the longest x1 0.28 us: body(): jnp.einsum('rqc,rcd->rqd', jnp.concatenate([high, low], axis=1), cached_v...]
    ppermute x0 -> x1, starting transfers between devices: none -> 2.06 us  [body(): other_table = lax.ppermute(embedding, 'core', [(0, 1), (1, 0)])]
    convert_element_type x4 -> x0, other arithmetic: 1.65 us -> none  [the longest x1 1.63 us: body(): new_value_weight.astype(jnp.bfloat16).reshape(own_rows, tp_size, HEAD_SIZE)]
    unnamed x15, local copies, waits for them, and re-layouts: 0.81 us -> 2.23 us
    all_to_all x4 -> x5, waiting for transfers between devices: 46.5 us -> 45.3 us  [the longest x1 14.9 us: body(): found = lax.all_to_all(found, 'z', split_axis=0, concat_axis=0, tiled=False)]
  transfers between devices with their start and end apart: 5 -> 6, of which waited for: 4 -> 5; matrix products, arithmetic and copies ran while one was open for 6% -> 6% of each run, Pallas kernels for 0% -> 0%
where the time goes in v2:
time: 117 us; the launch traced here: 116 us
  starting transfers between devices  46.1 us (39%)
  waiting for transfers between devices  45.3 us (39%)
  Pallas kernels  7.8 us (7%)
  blocking collectives  7.59 us (6%)
  other arithmetic  3.82 us (3%)
  local copies, waits for them, and re-layouts  3.63 us (3%)
    all_to_all x1, starting transfers between devices, body(): lax.all_to_all(own_ids, ('xh', 'z'), split_axis=0, concat_axis=0, tiled=F...  17 us
    all_to_all x1, waiting for transfers between devices, body(): found = lax.all_to_all(found, 'z', split_axis=0, concat_axis=0, tiled=False)  14.9 us
    all_to_all x1, waiting for transfers between devices, body(): lax.all_to_all(product, 'z', split_axis=0, concat_axis=0, tiled=False)  12.7 us
    all_to_all x1, starting transfers between devices, body(): found = lax.all_to_all(found, 'z', split_axis=0, concat_axis=0, tiled=False)  11.5 us
    all_to_all x1, waiting for transfers between devices, body(): lax.all_to_all(found, ('xh', TP), split_axis=0, concat_axis=0, tiled=False)  7.98 us
    pallas_call x5, Pallas kernels, call(): pl.pallas_call(kernel, out_shape=jax.ShapeDtypeStruct(shape, dtype), comp...  7.8 us
    all_gather x1, blocking collectives, body(): quad_rows = lax.all_gather(both, QUAD, axis=0, tiled=False)  7.59 us
    all_to_all x1, waiting for transfers between devices, body(): lax.all_to_all(packed, TP, split_axis=0, concat_axis=0, tiled=False)  6.11 us
  transfers between devices with their start and end apart: 6, of which 5 were waited for; matrix products, arithmetic and copies ran while one was open for 6% of the time, Pallas kernels for 0%

profile of v2, /device:TPU:2, one launch (start us, length us, event | category | flops | bytes accessed | tf_op | source)
XLA Modules:
  0.0 116.0 jit_solution(14429526896913596574)
XLA Ops:
  0.6 0.0 copy-start
  0.6 2.1 %collective-permute-start = (bf16[1280,640]{1,0:T(8,128)(2,1)}, bf16[1280,640]{1,0:T(8,128)(2,1)}, u32[]{:S(2)}, u32[]{:S(2)}) collective-permute-start(bf16[1280,640]{1,0:T(8,128)(2,1)} %table_ref.1), channel_id=1, source_target_pairs={{0,8},{8,0},{1,9},{9,1},{2,10},{10,2},{3,11},{11,3},{4,12},{12,4},... | collective-permute-start | bytes 4915208 | tf_op jit(solution)/shard_map/ppermute | solution.py:198
  2.7 0.8 copy.32
  3.5 0.1 broadcast_in_dim.18
  3.6 0.6 broadcast_in_dim.19
  4.2 17.0 %all-to-all-start = ((s32[32,1,8]{2,1,0:T(1,128)}), s32[32,1,8]{2,1,0:T(1,128)S(1)}, u32[]{:S(2)}, u32[]{:S(2)}) async-start(s32[32,1,8]{2,1,0:T(1,128)} %broadcast_in_dim.19), calls=%async_computation | async-start | bytes 32768 | tf_op jit(solution)/shard_map/all_to_all | solution.py:190
  21.2 1.9 %fusion.50 = (bf16[10,1024]{1,0:T(8,128)(2,1)S(1)}, f32[10,1024]{1,0:T(8,128)}, f32[10,1024]{1,0:T(8,128)}, f32[10,1024]{1,0:T(8,128)}, bf16[10,1024]{1,0:T(8,12...) fusion(f32[10,1024]{1,0:T(8,128)} %param.21, f32[10,1024]{1,0:T(8,128)} %param.22, ...), kind=kLoop, calls=%fused_computation.82 | loop fusion | flops 327680 | bytes 614400 | tf_op jit(solution)/shard_map/convert_element_type | solution.py:208
  23.2 0.1 pad_maximum_fusion
  23.3 0.1 add_multiply_fusion
  23.4 0.7 add_convert_fusion
  24.1 0.5 iota_compare_fusion
  24.6 7.6 %all_gather.3 = bf16[4,10,2048]{2,1,0:T(8,128)(2,1)S(1)} all-gather(bf16[1,10,2048]{2,1,0:T(8,128)(2,1)S(1)} %all_gather_reshape.3), channel_id=1, replica_groups=mesh['z'=16,'xh'=2,'core'=2,'tp'=8] {'xh','core'}, dimensions={0}, use_global_device_ids=true | all-gather | bytes 204800 | tf_op jit(solution)/shard_map/all_gather | solution.py:213
  32.2 0.1 reshape.159
  32.4 3.6 %all-to-all-done = s32[32,1,8]{2,1,0:T(1,128)S(1)} async-done(((s32[32,1,8]{2,1,0:T(1,128)}), s32[32,1,8]{2,1,0:T(1,128)S(1)}, u32[]{:S(2)}, u32[]{:S(2)}) %all-to-all-start) | async-done | bytes 1056 | tf_op jit(solution)/shard_map/all_to_all | solution.py:190
  36.0 0.1 sub.54
  36.1 0.1 broadcast_subtract_fusion.ids_ref
  36.2 0.0 collective-permute-done.other_ref
  36.2 1.4 %copy-done.1 = bf16[1280,640]{1,0:T(8,128)(2,1)S(1)} copy-done((bf16[1280,640]{1,0:T(8,128)(2,1)S(1)}, bf16[1280,640]{1,0:T(8,128)(2,1)}, u32[]{:S(2)}) %copy-start.1) | copy-done | bytes 1638424
  37.6 4.0 %shard_map.207 = bf16[256,768]{1,0:T(8,128)(2,1)} custom-call(s32[2,256]{1,0:T(2,128)S(1)} %broadcast_subtract_fusion.ids_ref, bf16[1280,640]{1,0:T(8,128)(2,1)S(1)} %copy-done.1, bf16[1280,640]{1,0:T(8,128)(2,1)} %collective-permute-done.other_ref, bf16[640,768]{1,0:T(8,128)(2,1)S(1)} %get-tuple-element.23.sort_ref), custom_call_target="tpu_custom_call" | custom-call | tf_op jit(solution)/shard_map/pallas_call | solution.py:40
  41.6 6.1 %all-to-all-start.1 = ((bf16[16,16,768]{2,1,0:T(8,128)(2,1)}), bf16[16,16,768]{2,1,0:T(8,128)(2,1)S(1)}, u32[]{:S(2)}, u32[]{:S(2)}) async-start(bf16[16,16,768]{2,1,0:T(8,128)(2,1)} %bitcast.4), calls=%async_computation.1 | async-start | bytes 786432 | tf_op jit(solution)/shard_map/all_to_all | solution.py:266
  47.7 0.0 copy-done.6
  47.7 0.0 copy-done.5
  47.7 0.1 iota_compare_fusion.1
  47.8 8.0 %all-to-all-done.1 = bf16[16,16,768]{2,1,0:T(8,128)(2,1)S(1)} async-done(((bf16[16,16,768]{2,1,0:T(8,128)(2,1)}), bf16[16,16,768]{2,1,0:T(8,128)(2,1)S(1)}, u32[]{:S(2)}, u32[]{:S(2)}) %all-to-all-start.1) | async-done | bytes 393248 | tf_op jit(solution)/shard_map/all_to_all | solution.py:266
  55.7 0.9 shard_map.208
  56.6 11.5 %all-to-all-start.2 = ((bf16[16,16,384]{2,1,0:T(8,128)(2,1)}), bf16[16,16,384]{2,1,0:T(8,128)(2,1)S(1)}, u32[]{:S(2)}, u32[]{:S(2)}) async-start(bf16[16,16,384]{2,1,0:T(8,128)(2,1)} %shard_map.208), calls=%async_computation.2 | async-start | bytes 393216 | tf_op jit(solution)/shard_map/all_to_all | solution.py:269
  68.2 0.1 convert_element_type.35
  68.2 0.0 copy-done.4
  68.2 0.1 reshape.162
  68.3 0.0 copy-done.3
  68.4 0.1 fusion.48
  68.5 0.2 fusion.4
  68.7 0.0 copy-done
  68.7 0.5 fusion.54
  69.1 14.9 %all-to-all-done.2.came_ref = bf16[16,16,384]{2,1,0:T(8,128)(2,1)S(1)} async-done(((bf16[16,16,384]{2,1,0:T(8,128)(2,1)}), bf16[16,16,384]{2,1,0:T(8,128)(2,1)S(1)}, u32[]{:S(2)}, u32[]{:S(2)}) %all-to-all-start.2) | async-done | bytes 196640 | tf_op jit(solution)/shard_map/all_to_all | solution.py:269
  84.0 0.8 shard_map.209
  84.8 4.8 %all-to-all-start.3 = ((bf16[8,144,128]{2,1,0:T(8,128)(2,1)}), bf16[8,144,128]{2,1,0:T(8,128)(2,1)S(1)}, u32[]{:S(2)}, u32[]{:S(2)}) async-start(bf16[8,144,128]{2,1,0:T(8,128)(2,1)} %shard_map.209), calls=%async_computation.3 | async-start | bytes 589824 | tf_op jit(solution)/shard_map/all_to_all | solution.py:272
  89.6 0.2 fusion.9
  89.8 6.1 %all-to-all-done.3.came_ref = bf16[8,144,128]{2,1,0:T(8,128)(2,1)S(1)} async-done(((bf16[8,144,128]{2,1,0:T(8,128)(2,1)}), bf16[8,144,128]{2,1,0:T(8,128)(2,1)S(1)}, u32[]{:S(2)}, u32[]{:S(2)}) %all-to-all-start.3) | async-done | bytes 294944 | tf_op jit(solution)/shard_map/all_to_all | solution.py:272
  95.9 0.9 shard_map.210
  96.8 4.6 %all-to-all-start.4 = ((f32[16,8,256]{2,1,0:T(8,128)}), f32[16,8,256]{2,1,0:T(8,128)S(1)}, u32[]{:S(2)}, u32[]{:S(2)}) async-start(f32[16,8,256]{2,1,0:T(8,128)} %shard_map.210), calls=%async_computation.4 | async-start | bytes 262144 | tf_op jit(solution)/shard_map/all_to_all | solution.py:274
  101.4 0.1 pad_maximum_fusion.1
  101.5 0.1 reshape_broadcast_in_dim.8.highest_ref
  101.6 0.1 reshape_broadcast_in_dim.9.sum_ref
  101.7 0.0 copy-done.2
  101.7 0.3 fusion.1
  102.0 12.7 %all-to-all-done.4.came_ref = f32[16,8,256]{2,1,0:T(8,128)S(1)} async-done(((f32[16,8,256]{2,1,0:T(8,128)}), f32[16,8,256]{2,1,0:T(8,128)S(1)}, u32[]{:S(2)}, u32[]{:S(2)}) %all-to-all-start.4) | async-done | bytes 131104 | tf_op jit(solution)/shard_map/all_to_all | solution.py:274
  114.7 1.3 %shard_map.211 = bf16[4,2,1024]{2,1,0:T(2,128)(2,1)} custom-call(f32[16,8,256]{2,1,0:T(8,128)S(1)} %all-to-all-done.4.came_ref, f32[1,128]{1,0:T(1,128)S(1)} %bitcast_convert_fusion.gain_ref, f32[8,128]{1,0:T(8,128)S(1)} %get-tuple-element.29.cosine_ref, f32[8,128]{1,0:T(8,128)S(1)} %get-tuple-element.30.sine_ref, ...), custom_call_target="tpu_custom_call" | custom-call | tf_op jit(solution)/shard_map/pallas_call | solution.py:40
  (18 shorter events, 0.2 us)
Async XLA Ops:
  0.6 68.0 %copy-start = (bf16[4,1,1024,128]{3,2,1,0:T(8,128)(2,1)S(1)}, bf16[4,1,1024,128]{3,2,1,0:T(8,128)(2,1)}, u32[]{:S(2)}) copy-start(bf16[4,1,1024,128]{3,2,1,0:T(8,128)(2,1)} %param.30) | copy-start | bytes 3145732
  0.6 35.5 %collective-permute-start = (bf16[1280,640]{1,0:T(8,128)(2,1)}, bf16[1280,640]{1,0:T(8,128)(2,1)}, u32[]{:S(2)}, u32[]{:S(2)}) collective-permute-start(bf16[1280,640]{1,0:T(8,128)(2,1)} %table_ref.1), channel_id=1, source_target_pairs={{0,8},{8,0},{1,9},{9,1},{2,10},{10,2},{3,11},{11,3},{4,12},{12,4},... | collective-permute-start | bytes 4915208 | tf_op jit(solution)/shard_map/ppermute | solution.py:198
  4.2 31.8 %all-to-all-start = ((s32[32,1,8]{2,1,0:T(1,128)}), s32[32,1,8]{2,1,0:T(1,128)S(1)}, u32[]{:S(2)}, u32[]{:S(2)}) async-start(s32[32,1,8]{2,1,0:T(1,128)} %broadcast_in_dim.19), calls=%async_computation | async-start | bytes 32768 | tf_op jit(solution)/shard_map/all_to_all | solution.py:190
  36.2 1.4 %copy-start.1 = (bf16[1280,640]{1,0:T(8,128)(2,1)S(1)}, bf16[1280,640]{1,0:T(8,128)(2,1)}, u32[]{:S(2)}) copy-start(bf16[1280,640]{1,0:T(8,128)(2,1)} %table_ref.1) | copy-start | bytes 4915204
  37.6 10.1 %copy-start.6 = (bf16[128]{0:T(256)(128)(2,1)S(1)}, bf16[128]{0:T(256)(128)(2,1)}, u32[]{:S(2)}) copy-start(bf16[128]{0:T(256)(128)(2,1)} %param.20) | copy-start | bytes 772
  37.6 10.1 %copy-start.5 = (s32[4]{0:T(128)S(1)}, s32[4]{0:T(128)}, u32[]{:S(2)}) copy-start(s32[4]{0:T(128)} %param.17) | copy-start | bytes 52
  41.6 26.7 %copy-start.4 = (bf16[5120]{0:T(1024)(128)(2,1)S(1)}, bf16[5120]{0:T(1024)(128)(2,1)}, u32[]{:S(2)}) copy-start(bf16[5120]{0:T(1024)(128)(2,1)} %param.19) | copy-start | bytes 30724
  41.6 26.8 %copy-start.3 = (bf16[4,2,1024]{2,1,0:T(2,128)(2,1)S(1)}, bf16[4,2,1024]{2,1,0:T(2,128)(2,1)}, u32[]{:S(2)}) copy-start(bf16[4,2,1024]{2,1,0:T(2,128)(2,1)} %param.29) | copy-start | bytes 49156
  41.6 14.2 %all-to-all-start.1 = ((bf16[16,16,768]{2,1,0:T(8,128)(2,1)}), bf16[16,16,768]{2,1,0:T(8,128)(2,1)S(1)}, u32[]{:S(2)}, u32[]{:S(2)}) async-start(bf16[16,16,768]{2,1,0:T(8,128)(2,1)} %bitcast.4), calls=%async_computation.1 | async-start | bytes 786432 | tf_op jit(solution)/shard_map/all_to_all | solution.py:266
  56.6 27.4 %all-to-all-start.2 = ((bf16[16,16,384]{2,1,0:T(8,128)(2,1)}), bf16[16,16,384]{2,1,0:T(8,128)(2,1)S(1)}, u32[]{:S(2)}, u32[]{:S(2)}) async-start(bf16[16,16,384]{2,1,0:T(8,128)(2,1)} %shard_map.208), calls=%async_computation.2 | async-start | bytes 393216 | tf_op jit(solution)/shard_map/all_to_all | solution.py:269
  69.1 32.5 %copy-start.2 = (bf16[4,1,1024,128]{3,2,1,0:T(8,128)(2,1)S(1)}, bf16[4,1,1024,128]{3,2,1,0:T(8,128)(2,1)}, u32[]{:S(2)}) copy-start(bf16[4,1,1024,128]{3,2,1,0:T(8,128)(2,1)} %param.31) | copy-start | bytes 3145732
  84.8 11.1 %all-to-all-start.3 = ((bf16[8,144,128]{2,1,0:T(8,128)(2,1)}), bf16[8,144,128]{2,1,0:T(8,128)(2,1)S(1)}, u32[]{:S(2)}, u32[]{:S(2)}) async-start(bf16[8,144,128]{2,1,0:T(8,128)(2,1)} %shard_map.209), calls=%async_computation.3 | async-start | bytes 589824 | tf_op jit(solution)/shard_map/all_to_all | solution.py:272
  96.8 17.9 %all-to-all-start.4 = ((f32[16,8,256]{2,1,0:T(8,128)}), f32[16,8,256]{2,1,0:T(8,128)S(1)}, u32[]{:S(2)}, u32[]{:S(2)}) async-start(f32[16,8,256]{2,1,0:T(8,128)} %shard_map.210), calls=%async_computation.4 | async-start | bytes 262144 | tf_op jit(solution)/shard_map/all_to_all | solution.py:274

commit v3 on v2

--- a/solution.py
+++ b/solution.py
@@ -11,6 +11,9 @@
 BLOCK_ROWS = 40
 BLOCK = 48
 CHUNK = 384
+OWN_ROWS = 10
+COVER_FLOPS = 20_000_000_000
+COVER_BYTES = 60_000_000
 HIGH_COLUMN = 40
 LOW_COLUMN = 41
 
@@ -44,31 +47,59 @@
     )(*operands)
 
 
-def look_up(ids_ref, table_ref, other_ref, sort_ref, found_ref):
-    count = ids_ref.shape[1]
+def look_up(row_ref, table_ref, other_ref, found_ref):
+    count = row_ref.shape[1]
     eye = lax.broadcasted_iota(jnp.int32, (count, count), 0) == lax.broadcasted_iota(
         jnp.int32, (count, count), 1
     )
-    total = jnp.zeros((count, table_ref.shape[1]), jnp.float32)
-    for part, held in enumerate((table_ref, other_ref)):
-        row = jnp.broadcast_to(ids_ref[part : part + 1, :], (count, count))
-        ids = jnp.sum(jnp.where(eye, row, 0), axis=1, keepdims=True)
-        index = lax.broadcasted_iota(jnp.int32, (count, held.shape[0]), 1)
-        onehot = jnp.where(ids == index, 1.0, 0.0).astype(jnp.bfloat16)
-        total += jnp.dot(onehot, held[...], preferred_element_type=jnp.float32)
-    found_ref[...] = jnp.dot(
-        total.astype(jnp.bfloat16), sort_ref[...], preferred_element_type=jnp.float32
-    ).astype(jnp.bfloat16)
-
-
-def split_rows(came_ref, chunks_ref):
+    row = jnp.broadcast_to(row_ref[...], (count, count))
+    row = jnp.sum(jnp.where(eye, row, 0), axis=1, keepdims=True)
+    size = table_ref.shape[0]
+    index = lax.broadcasted_iota(jnp.int32, (count, size), 1)
+    own = jnp.where(row == index, 1.0, 0.0).astype(jnp.bfloat16)
+    other = jnp.where(row - size == index, 1.0, 0.0).astype(jnp.bfloat16)
+    total = jnp.dot(own, table_ref[...], preferred_element_type=jnp.float32)
+    total += jnp.dot(other, other_ref[...], preferred_element_type=jnp.float32)
+    found_ref[...] = total.astype(jnp.bfloat16)
+
+
+def update(*refs):
+    given, new, both_ref = refs[:8], refs[8:14], refs[14]
+    for side in range(2):
+        results = adamw(*[ref[...] for ref in given[4 * side : 4 * side + 4]])
+        for ref, result in zip(new[3 * side : 3 * side + 3], results):
+            ref[...] = result
+        rounded = results[0].astype(jnp.bfloat16)
+        for place in range(rounded.shape[1] // HEAD_SIZE):
+            start = (2 * place + side) * HEAD_SIZE
+            both_ref[:, start : start + HEAD_SIZE] = rounded[
+                :, place * HEAD_SIZE : (place + 1) * HEAD_SIZE
+            ]
+
+
+def sort_columns(sort_ref):
+    features = sort_ref.shape[0]
+    column = lax.broadcasted_iota(jnp.int32, sort_ref.shape, 1)
+    half, place, row = column // CHUNK, column % CHUNK // BLOCK, column % BLOCK
+    quad, own = row // OWN_ROWS, row % OWN_ROWS
+    feature = half * (features // 2) + (quad * (CHUNK // BLOCK) + place) * OWN_ROWS + own
+    held = lax.broadcasted_iota(jnp.int32, sort_ref.shape, 0)
+    chosen = (held == feature) & (row < BLOCK_ROWS)
+    sort_ref[...] = jnp.where(chosen, 1.0, 0.0).astype(jnp.bfloat16)
+
+
+def split_rows(came_ref, sort_ref, chunks_ref):
     total = came_ref[0].astype(jnp.float32) + came_ref[1].astype(jnp.float32)
+    places, count, features = total.shape
     squares = jnp.sum(jnp.sum(total * total, axis=0), axis=-1, keepdims=True)
     high = squares.astype(jnp.bfloat16).astype(jnp.float32)
     low = squares - high
-    column = lax.broadcasted_iota(jnp.int32, (squares.shape[0], CHUNK), 1)
+    column = lax.broadcasted_iota(jnp.int32, (count, CHUNK), 1)
     extra = jnp.where(column == HIGH_COLUMN, high, jnp.where(column == LOW_COLUMN, low, 0.0))
-    for place in range(total.shape[0]):
+    total = total.reshape(places * count, features).astype(jnp.bfloat16)
+    total = jnp.dot(total, sort_ref[...], preferred_element_type=jnp.float32)
+    total = total.reshape(places, count, 2 * CHUNK)
+    for place in range(places):
         for half in range(2):
             chunk = total[place, :, half * CHUNK : (half + 1) * CHUNK] + extra
             chunks_ref[2 * place + half] = chunk.astype(jnp.bfloat16)
@@ -110,21 +141,22 @@
         ],
         axis=1,
     )
+    products = []
     for side in range(2):
         start = parts * count + side * BLOCK
         weight = came_ref[:, start : start + BLOCK, :].reshape(places * BLOCK, LANES)
         product = jnp.dot(normed, weight, preferred_element_type=jnp.float32)
-        product_ref[:, :, side * LANES : (side + 1) * LANES] = product.reshape(
-            product_ref.shape[0], product_ref.shape[1], LANES
-        )
+        products.append(product.reshape(product_ref.shape[0], product_ref.shape[1] // 2, LANES))
+    product_ref[...] = jnp.concatenate(products, axis=1).astype(jnp.bfloat16)
 
 
 def finish(
     came_ref, gain_ref, cosine_ref, sine_ref, query_ref, mixed_ref, highest_ref, sum_ref, out_ref
 ):
-    total = jnp.sum(came_ref[...], axis=0)
-    keys = total[:, :LANES]
-    values = total[:, LANES:].astype(jnp.bfloat16)
+    total = jnp.sum(came_ref[...].astype(jnp.float32), axis=0)
+    tokens = total.shape[0] // 2
+    keys = total[:tokens]
+    values = total[tokens:].astype(jnp.bfloat16)
     factor = lax.rsqrt(jnp.mean(keys * keys, axis=-1, keepdims=True) + norm_eps)
     keys = keys * factor * gain_ref[...]
     turned = jnp.concatenate([keys[:, LANES // 2 :], keys[:, : LANES // 2]], axis=1)
@@ -135,9 +167,10 @@
     ) * (HEAD_SIZE**-0.5)
     row = lax.broadcasted_iota(jnp.int32, fresh.shape, 0)
     column = lax.broadcasted_iota(jnp.int32, fresh.shape, 1)
-    each = count // (keys.shape[0] // 2)
+    each = count // (tokens // 2)
     step = row % each // (each // 2)
-    joined = (row // each == column // 2) & (column % 2 <= step)
+    rollouts = tokens // 2
+    joined = (row // each == column % rollouts) & (column // rollouts <= step)
     fresh = jnp.where(joined, fresh, -jnp.inf)
     highest = jnp.maximum(highest_ref[...], jnp.max(fresh, axis=-1, keepdims=True))
     weights = jnp.exp(fresh - highest)
@@ -186,35 +219,87 @@
     vocab_rows, features = embedding.shape
 
     chips = z_size * lax.axis_size("xh")
-    own_ids = jnp.broadcast_to(token_ids.reshape(1, tokens), (chips, tokens))
+    own_ids = jnp.broadcast_to(token_ids.T[None], (chips, 2, rollouts))
     all_ids = lax.all_to_all(own_ids, ("xh", "z"), split_axis=0, concat_axis=0, tiled=False)
 
-    column = jnp.arange(2 * CHUNK, dtype=jnp.int32)
-    half, place = column // CHUNK, column % CHUNK // BLOCK
-    row = column % BLOCK
-    feature = half * (features // 2) + (row // own_rows * tp_size + place) * own_rows + row % own_rows
-    feature = jnp.where(row < BLOCK_ROWS, feature, -1)
-    sort = (jnp.arange(features, dtype=jnp.int32)[:, None] == feature[None, :]).astype(jnp.bfloat16)
-    other_table = lax.ppermute(embedding, "core", [(0, 1), (1, 0)])
-
-    new_key_weight, new_key_first, new_key_second = adamw(
-        key_weight, key_grad, key_first, key_second
-    )
-    new_value_weight, new_value_first, new_value_second = adamw(
-        value_weight, value_grad, value_first, value_second
-    )
-    both = jnp.stack(
-        [
-            new_key_weight.astype(jnp.bfloat16).reshape(own_rows, tp_size, HEAD_SIZE),
-            new_value_weight.astype(jnp.bfloat16).reshape(own_rows, tp_size, HEAD_SIZE),
-        ],
-        axis=2,
-    ).reshape(own_rows, 2 * tp_size * HEAD_SIZE)
+    sort = pl.pallas_call(
+        sort_columns,
+        out_shape=jax.ShapeDtypeStruct((features, 2 * CHUNK), jnp.bfloat16),
+        compiler_params=pltpu.CompilerParams(vmem_limit_bytes=4 * 1024 * 1024),
+        cost_estimate=pl.CostEstimate(
+            flops=COVER_FLOPS, bytes_accessed=COVER_BYTES, transcendentals=0
+        ),
+    )()
+    all_ids, sort = lax.optimization_barrier((all_ids, sort))
+    other = lax.ppermute(embedding, "core", [(0, 1), (1, 0)])
+
+    part = lax.axis_index(FSDP)
+    ids = all_ids.reshape(1, -1)
+    own_row, other_row = ids - part * vocab_rows, ids - (part ^ 1) * vocab_rows
+    row = jnp.where((own_row >= 0) & (own_row < vocab_rows), own_row, -1)
+    row = jnp.where((other_row >= 0) & (other_row < vocab_rows), other_row + vocab_rows, row)
+    found = call(look_up, (row.shape[1], features), jnp.bfloat16, row, embedding, other)
+
+    (
+        found,
+        key_weight,
+        key_grad,
+        key_first,
+        key_second,
+        value_weight,
+        value_grad,
+        value_first,
+        value_second,
+        cache_lengths,
+        key_norm_gain,
+        norm_gain,
+    ) = lax.optimization_barrier(
+        (
+            found,
+            key_weight,
+            key_grad,
+            key_first,
+            key_second,
+            value_weight,
+            value_grad,
+            value_first,
+            value_second,
+            cache_lengths,
+            key_norm_gain,
+            norm_gain,
+        )
+    )
+
+    state = jax.ShapeDtypeStruct(key_weight.shape, jnp.float32)
+    (
+        new_key_weight,
+        new_key_first,
+        new_key_second,
+        new_value_weight,
+        new_value_first,
+        new_value_second,
+        both,
+    ) = pl.pallas_call(
+        update,
+        out_shape=[state] * 6
+        + [jax.ShapeDtypeStruct((own_rows, 2 * tp_size * HEAD_SIZE), jnp.bfloat16)],
+        compiler_params=pltpu.CompilerParams(vmem_limit_bytes=4 * 1024 * 1024),
+        cost_estimate=pl.CostEstimate(
+            flops=COVER_FLOPS, bytes_accessed=COVER_BYTES, transcendentals=0
+        ),
+    )(
+        key_weight,
+        key_grad,
+        key_first,
+        key_second,
+        value_weight,
+        value_grad,
+        value_first,
+        value_second,
+    )
     quad_rows = lax.all_gather(both, QUAD, axis=0, tiled=False)
     quad_rows = quad_rows.reshape(quad_size * own_rows, tp_size, 2 * HEAD_SIZE).transpose(1, 0, 2)
     quad_rows = jnp.pad(quad_rows, ((0, 0), (0, BLOCK - BLOCK_ROWS), (0, 0)))
-
-    all_ids, quad_rows = lax.optimization_barrier((all_ids, quad_rows))
 
     gain = jnp.dot(
         norm_gain.reshape(z_size, -1), sort[: features // 2, :CHUNK], preferred_element_type=jnp.float32
@@ -234,8 +319,9 @@
     cache_highest = jnp.max(cache_scores, axis=-1, keepdims=True)
     cache_exp = jnp.exp(cache_scores - cache_highest)
     cache_sum = jnp.sum(cache_exp, axis=-1, keepdims=True)
-    high = cache_exp.astype(jnp.bfloat16)
-    low = (cache_exp - high.astype(jnp.float32)).astype(jnp.bfloat16)
+    high = lax.reduce_precision(cache_exp, 8, 7)
+    low = (cache_exp - high).astype(jnp.bfloat16)
+    high = high.astype(jnp.bfloat16)
     cache_mixed = jnp.einsum(
         "rqc,rcd->rqd",
         jnp.concatenate([high, low], axis=1),
@@ -244,7 +330,7 @@
     )
     cache_mixed = cache_mixed[:, : 2 * groups] + cache_mixed[:, 2 * groups :]
 
-    positions = (cache_lengths[:, None] + jnp.arange(2, dtype=jnp.int32)[None, :]).astype(
+    positions = (cache_lengths[None, :] + jnp.arange(2, dtype=jnp.int32)[:, None]).astype(
         jnp.float32
     )
     frequency = rope_base ** (
@@ -255,22 +341,16 @@
     cosine = jnp.concatenate([cosine, cosine], axis=1)
     sine = jnp.concatenate([-sine, sine], axis=1)
 
-    part = lax.axis_index(FSDP)
-    owners = jnp.stack([part, part ^ 1])
-    ids = all_ids.reshape(1, -1) - owners[:, None] * vocab_rows
-    found = call(
-        look_up, (ids.shape[1], 2 * CHUNK), jnp.bfloat16, ids, embedding, other_table, sort
-    )
     each = 2 * tokens
-    found = found.reshape(-1, each, 2 * CHUNK)
+    found = found.reshape(-1, each, features)
     found = lax.all_to_all(found, ("xh", TP), split_axis=0, concat_axis=0, tiled=False)
-    found = found.reshape(2, tp_size, each, 2 * CHUNK)
-    found = call(split_rows, (z_size, each, CHUNK), jnp.bfloat16, found)
+    found = found.reshape(2, tp_size, each, features)
+    found = call(split_rows, (z_size, each, CHUNK), jnp.bfloat16, found, sort)
     found = lax.all_to_all(found, "z", split_axis=0, concat_axis=0, tiled=False)
     message_rows = CHUNK // LANES * each + 2 * BLOCK
     packed = call(pack, (tp_size, message_rows, LANES), jnp.bfloat16, found, quad_rows)
     packed = lax.all_to_all(packed, TP, split_axis=0, concat_axis=0, tiled=False)
-    product = call(project, (z_size, tokens, 2 * HEAD_SIZE), jnp.float32, packed, gain)
+    product = call(project, (z_size, 2 * tokens, HEAD_SIZE), jnp.bfloat16, packed, gain)
     product = lax.all_to_all(product, "z", split_axis=0, concat_axis=0, tiled=False)
     attention = call(
         finish,

time: 117 us -> 107 us (0.915)
  starting transfers between devices: 46.1 us -> 40.7 us
  other arithmetic: 3.82 us -> 0.58 us
  waiting for transfers between devices: 45.3 us -> 44 us
    all_to_all x1, waiting for transfers between devices: 3.63 us -> 11.8 us  [body(): lax.all_to_all(own_ids, ('xh', 'z'), split_axis=0, concat_axis=0, tiled=F...]
    all_to_all x1, waiting for transfers between devices: 14.9 us -> 7.09 us  [body(): found = lax.all_to_all(found, 'z', split_axis=0, concat_axis=0, tiled=False)]
    all_to_all x1, starting transfers between devices: 11.5 us -> 4.95 us  [body(): found = lax.all_to_all(found, 'z', split_axis=0, concat_axis=0, tiled=False)]
    convert_element_type x2 -> x1, other arithmetic: 2.59 us -> 0.01 us  [body(): (cache_lengths[None, :] + jnp.arange(2, dtype=jnp.int32)[:, None]).astype...]
    all_to_all x1, waiting for transfers between devices: 7.98 us -> 6.59 us  [body(): lax.all_to_all(found, ('xh', TP), split_axis=0, concat_axis=0, tiled=False)]
    all_to_all x1, starting transfers between devices: 4.56 us -> 5.91 us  [body(): lax.all_to_all(product, 'z', split_axis=0, concat_axis=0, tiled=False)]
  transfers between devices with their start and end apart: 6 -> 6, of which waited for: 5 -> 5; matrix products, arithmetic and copies ran while one was open for 6% -> 2% of each run, Pallas kernels for 0% -> 1%
where the time goes in v3:
time: 107 us; the launch traced here: 106 us
  waiting for transfers between devices  44 us (41%)
  starting transfers between devices  40.7 us (38%)
  Pallas kernels  8.63 us (8%)
  blocking collectives  7.29 us (7%)
  local copies, waits for them, and re-layouts  3.33 us (3%)
    all_to_all x1, starting transfers between devices, body(): lax.all_to_all(own_ids, ('xh', 'z'), split_axis=0, concat_axis=0, tiled=F...  17 us
    all_to_all x1, waiting for transfers between devices, body(): lax.all_to_all(product, 'z', split_axis=0, concat_axis=0, tiled=False)  12.5 us
    all_to_all x1, waiting for transfers between devices, body(): lax.all_to_all(own_ids, ('xh', 'z'), split_axis=0, concat_axis=0, tiled=F...  11.8 us
    pallas_call x5, Pallas kernels, call(): pl.pallas_call(kernel, out_shape=jax.ShapeDtypeStruct(shape, dtype), comp...  7.6 us
    all_gather x1, blocking collectives, body(): quad_rows = lax.all_gather(both, QUAD, axis=0, tiled=False)  7.29 us
    all_to_all x1, waiting for transfers between devices, body(): found = lax.all_to_all(found, 'z', split_axis=0, concat_axis=0, tiled=False)  7.09 us
    all_to_all x1, waiting for transfers between devices, body(): lax.all_to_all(found, ('xh', TP), split_axis=0, concat_axis=0, tiled=False)  6.59 us
    all_to_all x1, waiting for transfers between devices, body(): lax.all_to_all(packed, TP, split_axis=0, concat_axis=0, tiled=False)  6.01 us
  transfers between devices with their start and end apart: 6, of which 5 were waited for; matrix products, arithmetic and copies ran while one was open for 2% of the time, Pallas kernels for 1%

profile of v3, /device:TPU:2, one launch (start us, length us, event | category | flops | bytes accessed | tf_op | source)
XLA Modules:
  0.0 106.4 jit_solution(13982619727221998198)
XLA Ops:
  0.6 0.0 copy-start
  0.6 1.4 %broadcast_in_dim.18 = s32[32,2,4]{2,1,0:T(2,128)} broadcast(s32[2,4]{1,0:T(2,128)} %bitcast.25), dimensions={1,2} | broadcast | bytes 1056 | tf_op jit(solution)/shard_map/broadcast_in_dim | solution.py:222
  2.0 17.0 %all-to-all-start = ((s32[32,2,4]{2,1,0:T(2,128)}), s32[32,2,4]{2,1,0:T(2,128)S(1)}, u32[]{:S(2)}, u32[]{:S(2)}) async-start(s32[32,2,4]{2,1,0:T(2,128)} %broadcast_in_dim.18), calls=%async_computation | async-start | bytes 65536 | tf_op jit(solution)/shard_map/all_to_all | solution.py:223
  19.1 0.0 copy-start.13
  19.1 0.0 copy-start.1
  19.1 2.1 %collective-permute-start = (bf16[1280,640]{1,0:T(8,128)(2,1)}, bf16[1280,640]{1,0:T(8,128)(2,1)}, u32[]{:S(2)}, u32[]{:S(2)}) collective-permute-start(bf16[1280,640]{1,0:T(8,128)(2,1)} %table_ref.1), channel_id=1, source_target_pairs={{0,8},{8,0},{1,9},{9,1},{2,10},{10,2},{3,11},{11,3},{4,12},{12,4},... | collective-permute-start | bytes 4915208 | tf_op jit(solution)/shard_map/ppermute | solution.py:234
  21.2 0.2 shard_map.207.sort_ref
  21.4 1.0 copy-done.2
  22.4 11.8 %all-to-all-done = s32[32,2,4]{2,1,0:T(2,128)S(1)} async-done(((s32[32,2,4]{2,1,0:T(2,128)}), s32[32,2,4]{2,1,0:T(2,128)S(1)}, u32[]{:S(2)}, u32[]{:S(2)}) %all-to-all-start) | async-done | bytes 1056 | tf_op jit(solution)/shard_map/all_to_all | solution.py:223
  34.3 0.1 add.49
  34.4 0.1 sub.47
  34.6 0.1 and.29
  34.7 0.0 copy-start.15
  34.7 0.0 copy-start.4
  34.7 0.0 copy-start.5
  34.8 0.0 copy-start.6
  34.8 0.0 copy-start.8
  34.8 0.0 copy-start.9
  34.8 3.6 %shard_map.208 = bf16[256,640]{1,0:T(8,128)(2,1)} custom-call(s32[1,256]{1,0:T(1,128)S(1)} %fusion.11.row_ref, bf16[1280,640]{1,0:T(8,128)(2,1)S(1)} %copy-done.1, bf16[1280,640]{1,0:T(8,128)(2,1)} %collective-permute-done.other_ref), custom_call_target="tpu_custom_call" | custom-call | tf_op jit(solution)/shard_map/pallas_call | solution.py:43
  38.5 0.1 iota_compare_fusion
  38.6 6.0 %all-to-all-start.1 = ((bf16[16,16,640]{2,1,0:T(8,128)(2,1)}), bf16[16,16,640]{2,1,0:T(8,128)(2,1)S(1)}, u32[]{:S(2)}, u32[]{:S(2)}) async-start(bf16[16,16,640]{2,1,0:T(8,128)(2,1)} %bitcast.1), calls=%async_computation.1 | async-start | bytes 655360 | tf_op jit(solution)/shard_map/all_to_all | solution.py:346
  44.6 0.0 copy-start.16
  44.6 0.8 shard_map.210
  45.4 0.1 convert_element_type.20
  45.5 0.1 fusion.12
  45.6 6.6 %all-to-all-done.1 = bf16[16,16,640]{2,1,0:T(8,128)(2,1)S(1)} async-done(((bf16[16,16,640]{2,1,0:T(8,128)(2,1)}), bf16[16,16,640]{2,1,0:T(8,128)(2,1)S(1)}, u32[]{:S(2)}, u32[]{:S(2)}) %all-to-all-start.1) | async-done | bytes 327712 | tf_op jit(solution)/shard_map/all_to_all | solution.py:346
  52.2 1.0 shard_map.209
  53.2 5.0 %all-to-all-start.2 = ((bf16[16,16,384]{2,1,0:T(8,128)(2,1)}), bf16[16,16,384]{2,1,0:T(8,128)(2,1)S(1)}, u32[]{:S(2)}, u32[]{:S(2)}) async-start(bf16[16,16,384]{2,1,0:T(8,128)(2,1)} %shard_map.209), calls=%async_computation.2 | async-start | bytes 393216 | tf_op jit(solution)/shard_map/all_to_all | solution.py:349
  58.2 7.3 %all-gather.1 = bf16[4,10,2048]{2,1,0:T(8,128)(2,1)S(1)} all-gather(bf16[1,10,2048]{2,1,0:T(8,128)(2,1)S(1)} %bitcast.23), channel_id=2, replica_groups=mesh['z'=16,'xh'=2,'core'=2,'tp'=8] {'xh','core'}, dimensions={0}, use_global_device_ids=true | all-gather | bytes 204800 | tf_op jit(solution)/shard_map/all_gather | solution.py:300
  65.5 0.1 reshape.154
  65.6 0.1 reshape.155
  65.7 0.1 fusion.8
  65.9 0.0 copy-done
  65.9 0.0 copy-start.12
  65.9 0.5 fusion.14
  66.4 0.2 fusion.10
  66.6 7.1 %all-to-all-done.2.came_ref = bf16[16,16,384]{2,1,0:T(8,128)(2,1)S(1)} async-done(((bf16[16,16,384]{2,1,0:T(8,128)(2,1)}), bf16[16,16,384]{2,1,0:T(8,128)(2,1)S(1)}, u32[]{:S(2)}, u32[]{:S(2)}) %all-to-all-start.2) | async-done | bytes 196640 | tf_op jit(solution)/shard_map/all_to_all | solution.py:349
  73.7 0.8 shard_map.211
  74.5 4.8 %all-to-all-start.3 = ((bf16[8,144,128]{2,1,0:T(8,128)(2,1)}), bf16[8,144,128]{2,1,0:T(8,128)(2,1)S(1)}, u32[]{:S(2)}, u32[]{:S(2)}) async-start(bf16[8,144,128]{2,1,0:T(8,128)(2,1)} %shard_map.211), calls=%async_computation.3 | async-start | bytes 589824 | tf_op jit(solution)/shard_map/all_to_all | solution.py:352
  79.2 0.3 fusion.1
  79.5 6.0 %all-to-all-done.3.came_ref = bf16[8,144,128]{2,1,0:T(8,128)(2,1)S(1)} async-done(((bf16[8,144,128]{2,1,0:T(8,128)(2,1)}), bf16[8,144,128]{2,1,0:T(8,128)(2,1)S(1)}, u32[]{:S(2)}, u32[]{:S(2)}) %all-to-all-start.3) | async-done | bytes 294944 | tf_op jit(solution)/shard_map/all_to_all | solution.py:352
  85.5 0.9 shard_map.212
  86.4 5.9 %all-to-all-start.4 = ((bf16[16,16,128]{2,1,0:T(8,128)(2,1)}), bf16[16,16,128]{2,1,0:T(8,128)(2,1)S(1)}, u32[]{:S(2)}, u32[]{:S(2)}) async-start(bf16[16,16,128]{2,1,0:T(8,128)(2,1)} %shard_map.212), calls=%async_computation.4 | async-start | bytes 131072 | tf_op jit(solution)/shard_map/all_to_all | solution.py:354
  92.4 0.1 pad_maximum_fusion
  92.4 0.1 reshape_broadcast_in_dim.8.highest_ref
  92.5 0.1 reshape_broadcast_in_dim.9.sum_ref
  92.6 12.5 %all-to-all-done.4.came_ref = bf16[16,16,128]{2,1,0:T(8,128)(2,1)S(1)} async-done(((bf16[16,16,128]{2,1,0:T(8,128)(2,1)}), bf16[16,16,128]{2,1,0:T(8,128)(2,1)S(1)}, u32[]{:S(2)}, u32[]{:S(2)}) %all-to-all-start.4) | async-done | bytes 65568 | tf_op jit(solution)/shard_map/all_to_all | solution.py:354
  105.1 1.3 %shard_map.213 = bf16[4,2,1024]{2,1,0:T(2,128)(2,1)} custom-call(bf16[16,16,128]{2,1,0:T(8,128)(2,1)S(1)} %all-to-all-done.4.came_ref, f32[1,128]{1,0:T(1,128)S(1)} %bitcast_convert_fusion.gain_ref, f32[8,128]{1,0:T(8,128)S(1)} %get-tuple-element.59.cosine_ref, f32[8,128]{1,0:T(8,128)S(1)} %get-tuple-element.60.sine_ref, ...), custom_call_target="tpu_custom_call" | custom-call | tf_op jit(solution)/shard_map/pallas_call | solution.py:43
  (34 shorter events, 0.2 us)
Async XLA Ops:
  0.6 65.2 %copy-start = (bf16[4,1,1024,128]{3,2,1,0:T(8,128)(2,1)S(1)}, bf16[4,1,1024,128]{3,2,1,0:T(8,128)(2,1)}, u32[]{:S(2)}) copy-start(bf16[4,1,1024,128]{3,2,1,0:T(8,128)(2,1)} %param.30) | copy-start | bytes 3145732
  2.0 32.3 %all-to-all-start = ((s32[32,2,4]{2,1,0:T(2,128)}), s32[32,2,4]{2,1,0:T(2,128)S(1)}, u32[]{:S(2)}, u32[]{:S(2)}) async-start(s32[32,2,4]{2,1,0:T(2,128)} %broadcast_in_dim.18), calls=%async_computation | async-start | bytes 65536 | tf_op jit(solution)/shard_map/all_to_all | solution.py:223
  19.1 3.3 %copy-start.13 = (bf16[4,2,1024]{2,1,0:T(2,128)(2,1)S(1)}, bf16[4,2,1024]{2,1,0:T(2,128)(2,1)}, u32[]{:S(2)}) copy-start(bf16[4,2,1024]{2,1,0:T(2,128)(2,1)} %param.29) | copy-start | bytes 49156
  19.1 15.7 %copy-start.1 = (bf16[1280,640]{1,0:T(8,128)(2,1)S(1)}, bf16[1280,640]{1,0:T(8,128)(2,1)}, u32[]{:S(2)}) copy-start(bf16[1280,640]{1,0:T(8,128)(2,1)} %table_ref.1) | copy-start | bytes 4915204
  19.1 15.7 %collective-permute-start = (bf16[1280,640]{1,0:T(8,128)(2,1)}, bf16[1280,640]{1,0:T(8,128)(2,1)}, u32[]{:S(2)}, u32[]{:S(2)}) collective-permute-start(bf16[1280,640]{1,0:T(8,128)(2,1)} %table_ref.1), channel_id=1, source_target_pairs={{0,8},{8,0},{1,9},{9,1},{2,10},{10,2},{3,11},{11,3},{4,12},{12,4},... | collective-permute-start | bytes 4915208 | tf_op jit(solution)/shard_map/ppermute | solution.py:234
  21.4 1.0 copy-start.2
  34.7 3.8 %copy-start.15 = (s32[4]{0:T(128)S(1)}, s32[4]{0:T(128)}, u32[]{:S(2)}) copy-start(s32[4]{0:T(128)} %param.17) | copy-start | bytes 52
  34.7 9.8 %copy-start.4 = (f32[10,1024]{1,0:T(8,128)S(1)}, f32[10,1024]{1,0:T(8,128)}, u32[]{:S(2)}) copy-start(f32[10,1024]{1,0:T(8,128)} %refs_0_) | copy-start | bytes 122884
  34.7 9.8 %copy-start.5 = (f32[10,1024]{1,0:T(8,128)S(1)}, f32[10,1024]{1,0:T(8,128)}, u32[]{:S(2)}) copy-start(f32[10,1024]{1,0:T(8,128)} %refs_1_) | copy-start | bytes 122884
  34.8 9.8 %copy-start.6 = (f32[10,1024]{1,0:T(8,128)S(1)}, f32[10,1024]{1,0:T(8,128)}, u32[]{:S(2)}) copy-start(f32[10,1024]{1,0:T(8,128)} %refs_2_) | copy-start | bytes 122884
  34.8 9.8 %copy-start.7 = (f32[10,1024]{1,0:T(8,128)S(1)}, f32[10,1024]{1,0:T(8,128)}, u32[]{:S(2)}) copy-start(f32[10,1024]{1,0:T(8,128)} %refs_3_) | copy-start | bytes 122884
  34.8 9.8 %copy-start.8 = (f32[10,1024]{1,0:T(8,128)S(1)}, f32[10,1024]{1,0:T(8,128)}, u32[]{:S(2)}) copy-start(f32[10,1024]{1,0:T(8,128)} %refs_4_) | copy-start | bytes 122884
  34.8 9.8 %copy-start.9 = (f32[10,1024]{1,0:T(8,128)S(1)}, f32[10,1024]{1,0:T(8,128)}, u32[]{:S(2)}) copy-start(f32[10,1024]{1,0:T(8,128)} %refs_5_) | copy-start | bytes 122884
  34.8 9.8 %copy-start.10 = (f32[10,1024]{1,0:T(8,128)S(1)}, f32[10,1024]{1,0:T(8,128)}, u32[]{:S(2)}) copy-start(f32[10,1024]{1,0:T(8,128)} %refs_6_) | copy-start | bytes 122884
  34.8 9.8 %copy-start.11 = (f32[10,1024]{1,0:T(8,128)S(1)}, f32[10,1024]{1,0:T(8,128)}, u32[]{:S(2)}) copy-start(f32[10,1024]{1,0:T(8,128)} %refs_7_) | copy-start | bytes 122884
  38.6 13.6 %all-to-all-start.1 = ((bf16[16,16,640]{2,1,0:T(8,128)(2,1)}), bf16[16,16,640]{2,1,0:T(8,128)(2,1)S(1)}, u32[]{:S(2)}, u32[]{:S(2)}) async-start(bf16[16,16,640]{2,1,0:T(8,128)(2,1)} %bitcast.1), calls=%async_computation.1 | async-start | bytes 655360 | tf_op jit(solution)/shard_map/all_to_all | solution.py:346
  44.6 0.8 copy-start.16
  44.6 7.6 %copy-start.3 = (bf16[640,768]{1,0:T(8,128)(2,1)S(1)}, bf16[640,768]{1,0:T(8,128)(2,1)}, u32[]{:S(2)}) copy-start(bf16[640,768]{1,0:T(8,128)(2,1)} %copy-done.2) | copy-start | bytes 2949124
  45.4 20.2 %copy-start.14 = (bf16[5120]{0:T(1024)(128)(2,1)S(1)}, bf16[5120]{0:T(1024)(128)(2,1)}, u32[]{:S(2)}) copy-start(bf16[5120]{0:T(1024)(128)(2,1)} %param.19) | copy-start | bytes 30724
  53.2 20.5 %all-to-all-start.2 = ((bf16[16,16,384]{2,1,0:T(8,128)(2,1)}), bf16[16,16,384]{2,1,0:T(8,128)(2,1)S(1)}, u32[]{:S(2)}, u32[]{:S(2)}) async-start(bf16[16,16,384]{2,1,0:T(8,128)(2,1)} %shard_map.209), calls=%async_computation.2 | async-start | bytes 393216 | tf_op jit(solution)/shard_map/all_to_all | solution.py:349
  65.9 13.4 %copy-start.12 = (bf16[4,1,1024,128]{3,2,1,0:T(8,128)(2,1)S(1)}, bf16[4,1,1024,128]{3,2,1,0:T(8,128)(2,1)}, u32[]{:S(2)}) copy-start(bf16[4,1,1024,128]{3,2,1,0:T(8,128)(2,1)} %param.31) | copy-start | bytes 3145732
  74.5 11.1 %all-to-all-start.3 = ((bf16[8,144,128]{2,1,0:T(8,128)(2,1)}), bf16[8,144,128]{2,1,0:T(8,128)(2,1)S(1)}, u32[]{:S(2)}, u32[]{:S(2)}) async-start(bf16[8,144,128]{2,1,0:T(8,128)(2,1)} %shard_map.211), calls=%async_computation.3 | async-start | bytes 589824 | tf_op jit(solution)/shard_map/all_to_all | solution.py:352
  86.4 18.7 %all-to-all-start.4 = ((bf16[16,16,128]{2,1,0:T(8,128)(2,1)}), bf16[16,16,128]{2,1,0:T(8,128)(2,1)S(1)}, u32[]{:S(2)}, u32[]{:S(2)}) async-start(bf16[16,16,128]{2,1,0:T(8,128)(2,1)} %shard_map.212), calls=%async_computation.4 | async-start | bytes 131072 | tf_op jit(solution)/shard_map/all_to_all | solution.py:354

commit v4 on v3

--- a/solution.py
+++ b/solution.py
@@ -297,10 +297,7 @@
         value_first,
         value_second,
     )
-    quad_rows = lax.all_gather(both, QUAD, axis=0, tiled=False)
-    quad_rows = quad_rows.reshape(quad_size * own_rows, tp_size, 2 * HEAD_SIZE).transpose(1, 0, 2)
-    quad_rows = jnp.pad(quad_rows, ((0, 0), (0, BLOCK - BLOCK_ROWS), (0, 0)))
-
+    pair_rows = lax.all_gather(both, "core", axis=0, tiled=False)
     gain = jnp.dot(
         norm_gain.reshape(z_size, -1), sort[: features // 2, :CHUNK], preferred_element_type=jnp.float32
     )
@@ -344,6 +341,11 @@
     each = 2 * tokens
     found = found.reshape(-1, each, features)
     found = lax.all_to_all(found, ("xh", TP), split_axis=0, concat_axis=0, tiled=False)
+    found, pair_rows = lax.optimization_barrier((found, pair_rows))
+    quad_rows = lax.all_gather(pair_rows, "xh", axis=0, tiled=False)
+    quad_rows = quad_rows.reshape(quad_size * own_rows, tp_size, 2 * HEAD_SIZE).transpose(1, 0, 2)
+    quad_rows = jnp.pad(quad_rows, ((0, 0), (0, BLOCK - BLOCK_ROWS), (0, 0)))
+
     found = found.reshape(2, tp_size, each, features)
     found = call(split_rows, (z_size, each, CHUNK), jnp.bfloat16, found, sort)
     found = lax.all_to_all(found, "z", split_axis=0, concat_axis=0, tiled=False)

time: 107 us -> 106 us (level)
  blocking collectives: 7.29 us -> 9.16 us
  waiting for transfers between devices: 44 us -> 42.3 us
  starting transfers between devices: 40.7 us -> 39.6 us
    all_to_all x1, waiting for transfers between devices: 6.59 us -> 4.49 us  [body(): lax.all_to_all(found, ('xh', TP), split_axis=0, concat_axis=0, tiled=False)]
    all_gather x1 -> x2, blocking collectives: 7.29 us -> 9.16 us  [the longest x1 7.27 us: body(): quad_rows = lax.all_gather(pair_rows, 'xh', axis=0, tiled=False)]
    all_to_all x1, starting transfers between devices: 5.91 us -> 4.84 us  [body(): lax.all_to_all(product, 'z', split_axis=0, concat_axis=0, tiled=False)]
where the time goes in v4:
time: 106 us; the launch traced here: 105 us
  waiting for transfers between devices  42.3 us (40%)
  starting transfers between devices  39.6 us (37%)
  blocking collectives  9.16 us (9%)
  Pallas kernels  8.63 us (8%)
  local copies, waits for them, and re-layouts  3.32 us (3%)
    all_to_all x1, starting transfers between devices, body(): lax.all_to_all(own_ids, ('xh', 'z'), split_axis=0, concat_axis=0, tiled=F...  17 us
    all_to_all x1, waiting for transfers between devices, body(): lax.all_to_all(product, 'z', split_axis=0, concat_axis=0, tiled=False)  12.6 us
    all_to_all x1, waiting for transfers between devices, body(): lax.all_to_all(own_ids, ('xh', 'z'), split_axis=0, concat_axis=0, tiled=F...  11.8 us
    pallas_call x5, Pallas kernels, call(): pl.pallas_call(kernel, out_shape=jax.ShapeDtypeStruct(shape, dtype), comp...  7.61 us
    all_to_all x1, waiting for transfers between devices, body(): found = lax.all_to_all(found, 'z', split_axis=0, concat_axis=0, tiled=False)  7.32 us
    all_gather x1, blocking collectives, body(): quad_rows = lax.all_gather(pair_rows, 'xh', axis=0, tiled=False)  7.27 us
    all_to_all x1, waiting for transfers between devices, body(): lax.all_to_all(packed, TP, split_axis=0, concat_axis=0, tiled=False)  6 us
    all_to_all x1, starting transfers between devices, body(): lax.all_to_all(found, ('xh', TP), split_axis=0, concat_axis=0, tiled=False)  5.94 us
  transfers between devices with their start and end apart: 6, of which 5 were waited for; matrix products, arithmetic and copies ran while one was open for 2% of the time, Pallas kernels for 1%

profile of v4, /device:TPU:2, one launch (start us, length us, event | category | flops | bytes accessed | tf_op | source)
XLA Modules:
  0.0 105.5 jit_solution(17545878535597411098)
XLA Ops:
  0.6 0.0 copy-start
  0.6 1.4 %broadcast_in_dim.18 = s32[32,2,4]{2,1,0:T(2,128)} broadcast(s32[2,4]{1,0:T(2,128)} %bitcast.25), dimensions={1,2} | broadcast | bytes 1056 | tf_op jit(solution)/shard_map/broadcast_in_dim | solution.py:222
  2.0 17.0 %all-to-all-start = ((s32[32,2,4]{2,1,0:T(2,128)}), s32[32,2,4]{2,1,0:T(2,128)S(1)}, u32[]{:S(2)}, u32[]{:S(2)}) async-start(s32[32,2,4]{2,1,0:T(2,128)} %broadcast_in_dim.18), calls=%async_computation | async-start | bytes 65536 | tf_op jit(solution)/shard_map/all_to_all | solution.py:223
  19.1 0.0 copy-start.13
  19.1 0.0 copy-start.1
  19.1 2.1 %collective-permute-start = (bf16[1280,640]{1,0:T(8,128)(2,1)}, bf16[1280,640]{1,0:T(8,128)(2,1)}, u32[]{:S(2)}, u32[]{:S(2)}) collective-permute-start(bf16[1280,640]{1,0:T(8,128)(2,1)} %table_ref.1), channel_id=1, source_target_pairs={{0,8},{8,0},{1,9},{9,1},{2,10},{10,2},{3,11},{11,3},{4,12},{12,4},... | collective-permute-start | bytes 4915208 | tf_op jit(solution)/shard_map/ppermute | solution.py:234
  21.2 0.2 shard_map.207.sort_ref
  21.4 1.0 copy-done.2
  22.4 11.8 %all-to-all-done = s32[32,2,4]{2,1,0:T(2,128)S(1)} async-done(((s32[32,2,4]{2,1,0:T(2,128)}), s32[32,2,4]{2,1,0:T(2,128)S(1)}, u32[]{:S(2)}, u32[]{:S(2)}) %all-to-all-start) | async-done | bytes 1056 | tf_op jit(solution)/shard_map/all_to_all | solution.py:223
  34.3 0.1 add.49
  34.4 0.1 sub.47
  34.6 0.1 and.29
  34.7 0.0 copy-start.15
  34.7 0.0 copy-start.4
  34.7 0.0 copy-start.5
  34.8 0.0 copy-start.6
  34.8 0.0 copy-start.7
  34.8 0.0 copy-start.10
  34.8 0.0 copy-start.11
  34.8 3.6 %shard_map.208 = bf16[256,640]{1,0:T(8,128)(2,1)} custom-call(s32[1,256]{1,0:T(1,128)S(1)} %fusion.11.row_ref, bf16[1280,640]{1,0:T(8,128)(2,1)S(1)} %copy-done.1, bf16[1280,640]{1,0:T(8,128)(2,1)} %collective-permute-done.other_ref), custom_call_target="tpu_custom_call" | custom-call | tf_op jit(solution)/shard_map/pallas_call | solution.py:43
  38.5 0.1 convert_element_type.20
  38.6 5.9 %all-to-all-start.1 = ((bf16[16,16,640]{2,1,0:T(8,128)(2,1)}), bf16[16,16,640]{2,1,0:T(8,128)(2,1)S(1)}, u32[]{:S(2)}, u32[]{:S(2)}) async-start(bf16[16,16,640]{2,1,0:T(8,128)(2,1)} %bitcast.1), calls=%async_computation.1 | async-start | bytes 655360 | tf_op jit(solution)/shard_map/all_to_all | solution.py:343
  44.5 0.1 fusion.12
  44.7 0.0 copy-start.14
  44.7 0.8 shard_map.209
  45.5 0.1 iota_compare_fusion
  45.6 0.1 reshape.155
  45.7 1.9 %all-gather.2 = bf16[2,10,2048]{2,1,0:T(8,128)(2,1)S(1)} all-gather(bf16[1,10,2048]{2,1,0:T(8,128)(2,1)S(1)} %bitcast.23), channel_id=2, replica_groups=mesh['z'=16,'xh'=2,'core'=2,'tp'=8] {'core'}, dimensions={0}, use_global_device_ids=true | all-gather | bytes 122880 | tf_op jit(solution)/shard_map/all_gather | solution.py:300
  47.6 0.1 fusion.8
  47.7 4.5 %all-to-all-done.1 = bf16[16,16,640]{2,1,0:T(8,128)(2,1)S(1)} async-done(((bf16[16,16,640]{2,1,0:T(8,128)(2,1)}), bf16[16,16,640]{2,1,0:T(8,128)(2,1)S(1)}, u32[]{:S(2)}, u32[]{:S(2)}) %all-to-all-start.1) | async-done | bytes 327712 | tf_op jit(solution)/shard_map/all_to_all | solution.py:343
  52.2 1.0 shard_map.210
  53.2 5.0 %all-to-all-start.2 = ((bf16[16,16,384]{2,1,0:T(8,128)(2,1)}), bf16[16,16,384]{2,1,0:T(8,128)(2,1)S(1)}, u32[]{:S(2)}, u32[]{:S(2)}) async-start(bf16[16,16,384]{2,1,0:T(8,128)(2,1)} %shard_map.210), calls=%async_computation.2 | async-start | bytes 393216 | tf_op jit(solution)/shard_map/all_to_all | solution.py:351
  58.2 0.5 fusion.14
  58.7 0.2 fusion.10
  58.9 7.3 %all-gather.1 = bf16[4,10,2048]{2,1,0:T(8,128)(2,1)S(1)} all-gather(bf16[2,10,2048]{2,1,0:T(8,128)(2,1)S(1)} %all-gather.2), channel_id=3, replica_groups=mesh['z'=16,'xh'=2,'core'=2,'tp'=8] {'xh'}, dimensions={0}, use_global_device_ids=true | all-gather | bytes 245760 | tf_op jit(solution)/shard_map/all_gather | solution.py:345
  66.2 0.1 reshape.154
  66.4 7.3 %all-to-all-done.2.came_ref = bf16[16,16,384]{2,1,0:T(8,128)(2,1)S(1)} async-done(((bf16[16,16,384]{2,1,0:T(8,128)(2,1)}), bf16[16,16,384]{2,1,0:T(8,128)(2,1)S(1)}, u32[]{:S(2)}, u32[]{:S(2)}) %all-to-all-start.2) | async-done | bytes 196640 | tf_op jit(solution)/shard_map/all_to_all | solution.py:351
  73.7 0.8 shard_map.211
  74.5 4.8 %all-to-all-start.3 = ((bf16[8,144,128]{2,1,0:T(8,128)(2,1)}), bf16[8,144,128]{2,1,0:T(8,128)(2,1)S(1)}, u32[]{:S(2)}, u32[]{:S(2)}) async-start(bf16[8,144,128]{2,1,0:T(8,128)(2,1)} %shard_map.211), calls=%async_computation.3 | async-start | bytes 589824 | tf_op jit(solution)/shard_map/all_to_all | solution.py:354
  79.2 0.3 fusion.1
  79.5 6.0 %all-to-all-done.3.came_ref = bf16[8,144,128]{2,1,0:T(8,128)(2,1)S(1)} async-done(((bf16[8,144,128]{2,1,0:T(8,128)(2,1)}), bf16[8,144,128]{2,1,0:T(8,128)(2,1)S(1)}, u32[]{:S(2)}, u32[]{:S(2)}) %all-to-all-start.3) | async-done | bytes 294944 | tf_op jit(solution)/shard_map/all_to_all | solution.py:354
  85.5 0.9 shard_map.212
  86.4 4.8 %all-to-all-start.4 = ((bf16[16,16,128]{2,1,0:T(8,128)(2,1)}), bf16[16,16,128]{2,1,0:T(8,128)(2,1)S(1)}, u32[]{:S(2)}, u32[]{:S(2)}) async-start(bf16[16,16,128]{2,1,0:T(8,128)(2,1)} %shard_map.212), calls=%async_computation.4 | async-start | bytes 131072 | tf_op jit(solution)/shard_map/all_to_all | solution.py:356
  91.3 0.1 pad_maximum_fusion
  91.4 0.1 reshape_broadcast_in_dim.8.highest_ref
  91.5 0.1 reshape_broadcast_in_dim.9.sum_ref
  91.6 12.6 %all-to-all-done.4.came_ref = bf16[16,16,128]{2,1,0:T(8,128)(2,1)S(1)} async-done(((bf16[16,16,128]{2,1,0:T(8,128)(2,1)}), bf16[16,16,128]{2,1,0:T(8,128)(2,1)S(1)}, u32[]{:S(2)}, u32[]{:S(2)}) %all-to-all-start.4) | async-done | bytes 65568 | tf_op jit(solution)/shard_map/all_to_all | solution.py:356
  104.2 1.3 %shard_map.213 = bf16[4,2,1024]{2,1,0:T(2,128)(2,1)} custom-call(bf16[16,16,128]{2,1,0:T(8,128)(2,1)S(1)} %all-to-all-done.4.came_ref, f32[1,128]{1,0:T(1,128)S(1)} %bitcast_convert_fusion.gain_ref, f32[8,128]{1,0:T(8,128)S(1)} %get-tuple-element.63.cosine_ref, f32[8,128]{1,0:T(8,128)S(1)} %get-tuple-element.64.sine_ref, ...), custom_call_target="tpu_custom_call" | custom-call | tf_op jit(solution)/shard_map/pallas_call | solution.py:43
  (35 shorter events, 0.2 us)
Async XLA Ops:
  0.6 57.6 %copy-start = (bf16[4,1,1024,128]{3,2,1,0:T(8,128)(2,1)S(1)}, bf16[4,1,1024,128]{3,2,1,0:T(8,128)(2,1)}, u32[]{:S(2)}) copy-start(bf16[4,1,1024,128]{3,2,1,0:T(8,128)(2,1)} %param.30) | copy-start | bytes 3145732
  2.0 32.3 %all-to-all-start = ((s32[32,2,4]{2,1,0:T(2,128)}), s32[32,2,4]{2,1,0:T(2,128)S(1)}, u32[]{:S(2)}, u32[]{:S(2)}) async-start(s32[32,2,4]{2,1,0:T(2,128)} %broadcast_in_dim.18), calls=%async_computation | async-start | bytes 65536 | tf_op jit(solution)/shard_map/all_to_all | solution.py:223
  19.1 3.3 %copy-start.13 = (bf16[4,2,1024]{2,1,0:T(2,128)(2,1)S(1)}, bf16[4,2,1024]{2,1,0:T(2,128)(2,1)}, u32[]{:S(2)}) copy-start(bf16[4,2,1024]{2,1,0:T(2,128)(2,1)} %param.29) | copy-start | bytes 49156
  19.1 15.7 %copy-start.1 = (bf16[1280,640]{1,0:T(8,128)(2,1)S(1)}, bf16[1280,640]{1,0:T(8,128)(2,1)}, u32[]{:S(2)}) copy-start(bf16[1280,640]{1,0:T(8,128)(2,1)} %table_ref.1) | copy-start | bytes 4915204
  19.1 15.7 %collective-permute-start = (bf16[1280,640]{1,0:T(8,128)(2,1)}, bf16[1280,640]{1,0:T(8,128)(2,1)}, u32[]{:S(2)}, u32[]{:S(2)}) collective-permute-start(bf16[1280,640]{1,0:T(8,128)(2,1)} %table_ref.1), channel_id=1, source_target_pairs={{0,8},{8,0},{1,9},{9,1},{2,10},{10,2},{3,11},{11,3},{4,12},{12,4},... | collective-permute-start | bytes 4915208 | tf_op jit(solution)/shard_map/ppermute | solution.py:234
  21.4 1.0 copy-start.2
  34.7 3.8 %copy-start.15 = (s32[4]{0:T(128)S(1)}, s32[4]{0:T(128)}, u32[]{:S(2)}) copy-start(s32[4]{0:T(128)} %param.17) | copy-start | bytes 52
  34.7 9.9 %copy-start.4 = (f32[10,1024]{1,0:T(8,128)S(1)}, f32[10,1024]{1,0:T(8,128)}, u32[]{:S(2)}) copy-start(f32[10,1024]{1,0:T(8,128)} %refs_0_) | copy-start | bytes 122884
  34.7 9.9 %copy-start.5 = (f32[10,1024]{1,0:T(8,128)S(1)}, f32[10,1024]{1,0:T(8,128)}, u32[]{:S(2)}) copy-start(f32[10,1024]{1,0:T(8,128)} %refs_1_) | copy-start | bytes 122884
  34.8 9.9 %copy-start.6 = (f32[10,1024]{1,0:T(8,128)S(1)}, f32[10,1024]{1,0:T(8,128)}, u32[]{:S(2)}) copy-start(f32[10,1024]{1,0:T(8,128)} %refs_2_) | copy-start | bytes 122884
  34.8 9.9 %copy-start.7 = (f32[10,1024]{1,0:T(8,128)S(1)}, f32[10,1024]{1,0:T(8,128)}, u32[]{:S(2)}) copy-start(f32[10,1024]{1,0:T(8,128)} %refs_3_) | copy-start | bytes 122884
  34.8 9.9 %copy-start.8 = (f32[10,1024]{1,0:T(8,128)S(1)}, f32[10,1024]{1,0:T(8,128)}, u32[]{:S(2)}) copy-start(f32[10,1024]{1,0:T(8,128)} %refs_4_) | copy-start | bytes 122884
  34.8 9.9 %copy-start.9 = (f32[10,1024]{1,0:T(8,128)S(1)}, f32[10,1024]{1,0:T(8,128)}, u32[]{:S(2)}) copy-start(f32[10,1024]{1,0:T(8,128)} %refs_5_) | copy-start | bytes 122884
  34.8 9.9 %copy-start.10 = (f32[10,1024]{1,0:T(8,128)S(1)}, f32[10,1024]{1,0:T(8,128)}, u32[]{:S(2)}) copy-start(f32[10,1024]{1,0:T(8,128)} %refs_6_) | copy-start | bytes 122884
  34.8 9.9 %copy-start.11 = (f32[10,1024]{1,0:T(8,128)S(1)}, f32[10,1024]{1,0:T(8,128)}, u32[]{:S(2)}) copy-start(f32[10,1024]{1,0:T(8,128)} %refs_7_) | copy-start | bytes 122884
  38.6 13.6 %all-to-all-start.1 = ((bf16[16,16,640]{2,1,0:T(8,128)(2,1)}), bf16[16,16,640]{2,1,0:T(8,128)(2,1)S(1)}, u32[]{:S(2)}, u32[]{:S(2)}) async-start(bf16[16,16,640]{2,1,0:T(8,128)(2,1)} %bitcast.1), calls=%async_computation.1 | async-start | bytes 655360 | tf_op jit(solution)/shard_map/all_to_all | solution.py:343
  44.7 0.9 copy-start.14
  44.7 2.9 %copy-start.3 = (bf16[640,768]{1,0:T(8,128)(2,1)S(1)}, bf16[640,768]{1,0:T(8,128)(2,1)}, u32[]{:S(2)}) copy-start(bf16[640,768]{1,0:T(8,128)(2,1)} %copy-done.2) | copy-start | bytes 2949124
  45.5 12.7 %copy-start.16 = (bf16[128]{0:T(256)(128)(2,1)S(1)}, bf16[128]{0:T(256)(128)(2,1)}, u32[]{:S(2)}) copy-start(bf16[128]{0:T(256)(128)(2,1)} %param.20) | copy-start | bytes 772
  53.2 20.5 %all-to-all-start.2 = ((bf16[16,16,384]{2,1,0:T(8,128)(2,1)}), bf16[16,16,384]{2,1,0:T(8,128)(2,1)S(1)}, u32[]{:S(2)}, u32[]{:S(2)}) async-start(bf16[16,16,384]{2,1,0:T(8,128)(2,1)} %shard_map.210), calls=%async_computation.2 | async-start | bytes 393216 | tf_op jit(solution)/shard_map/all_to_all | solution.py:351
  58.7 20.6 %copy-start.12 = (bf16[4,1,1024,128]{3,2,1,0:T(8,128)(2,1)S(1)}, bf16[4,1,1024,128]{3,2,1,0:T(8,128)(2,1)}, u32[]{:S(2)}) copy-start(bf16[4,1,1024,128]{3,2,1,0:T(8,128)(2,1)} %param.31) | copy-start | bytes 3145732
  74.5 11.1 %all-to-all-start.3 = ((bf16[8,144,128]{2,1,0:T(8,128)(2,1)}), bf16[8,144,128]{2,1,0:T(8,128)(2,1)S(1)}, u32[]{:S(2)}, u32[]{:S(2)}) async-start(bf16[8,144,128]{2,1,0:T(8,128)(2,1)} %shard_map.211), calls=%async_computation.3 | async-start | bytes 589824 | tf_op jit(solution)/shard_map/all_to_all | solution.py:354
  86.4 17.7 %all-to-all-start.4 = ((bf16[16,16,128]{2,1,0:T(8,128)(2,1)}), bf16[16,16,128]{2,1,0:T(8,128)(2,1)S(1)}, u32[]{:S(2)}, u32[]{:S(2)}) async-start(bf16[16,16,128]{2,1,0:T(8,128)(2,1)} %shard_map.212), calls=%async_computation.4 | async-start | bytes 131072 | tf_op jit(solution)/shard_map/all_to_all | solution.py:356
